TPU v7x, 512 devices: a whole 4x8x8 slice. The times are simulated.
512 devices in a mesh: rep: 16 (over y_hi, x, core), fsdp: 32 (over z, y_lo).
Axes of the slice: x: 4, y: 8 (y_hi: 2, y_lo: 4; y = y_hi * 4 + y_lo), z: 8, core: 2. Of those that a mesh axis runs over, the one named last changes fastest.
Arguments:
- grads: float32 [16, 256, 16384], P('rep', 'fsdp'), may hold values from -6 to 6
- master: float32 [256, 16384], P('fsdp'), may hold values from -6 to 6
- moment_one: float32 [256, 16384], P('fsdp'), may hold values from -2 to 2
- moment_two: float32 [256, 16384], P('fsdp'), may hold values from 0.05 to 2
Outputs:
- new_master: float32 [256, 16384], P('fsdp')
- new_one: float32 [256, 16384], P('fsdp')
- new_two: float32 [256, 16384], P('fsdp')
- rollout: bfloat16 [256, 16384], P(None, 'fsdp')
All inputs are finite; a program needn't handle non-finite values.
Results may differ from a plain program's by a relative error of at most 0.0025.
Values may be sent and summed in bfloat16 or wider, within the bound.
No kernel may reach another device: no remote copies, remote signals or barrier semaphores. Data moves between devices by JAX's collectives and lax.ppermute only.
A program may use at most 64 MiB of HBM per device.

v0:
```python
import jax
import jax.numpy as jnp
from jax import lax
from jax.sharding import PartitionSpec as P

STEP = 10


def adamw(mean_grad, master, moment_one, moment_two):
    new_one = 0.9 * moment_one + 0.1 * mean_grad
    new_two = 0.95 * moment_two + 0.05 * mean_grad * mean_grad
    corrected_one = new_one / (1.0 - 0.9**STEP)
    corrected_two = new_two / (1.0 - 0.95**STEP)
    new_master = master - 0.02 * (corrected_one / (jnp.sqrt(corrected_two) + 1e-08) + 0.1 * master)
    return (new_master, new_one, new_two)


def local(grads, master, moment_one, moment_two):
    row_count, full_width = master.shape
    fsdp_count = lax.axis_size("fsdp")
    rep_count = lax.axis_size("rep")
    piece_width = full_width // fsdp_count
    block_count = 1
    block_width = piece_width // block_count

    def columns(source):
        viewed = source.reshape(row_count, fsdp_count, piece_width)
        return viewed.reshape(row_count, fsdp_count * block_width)

    masters, firsts, seconds, rollouts = ([], [], [], [])
    grad_block = columns(grads[0])
    master_block = columns(master)
    first_block = columns(moment_one)
    second_block = columns(moment_two)
    mean_grad = lax.psum(grad_block.astype(jnp.bfloat16), "rep").astype(jnp.float32) / rep_count
    new_master, new_one, new_two = adamw(mean_grad, master_block, first_block, second_block)
    fresh = lax.all_to_all(
        new_master.astype(jnp.bfloat16), "fsdp", split_axis=1, concat_axis=0, tiled=True
    )
    masters.append(new_master.reshape(row_count, fsdp_count, block_width))
    firsts.append(new_one.reshape(row_count, fsdp_count, block_width))
    seconds.append(new_two.reshape(row_count, fsdp_count, block_width))
    rollouts.append(fresh)

    def assemble(pieces):
        return pieces[0].reshape(row_count, full_width)

    rollout = rollouts[0]
    return (assemble(masters), assemble(firsts), assemble(seconds), rollout)


def solution(mesh):
    placed = (P("rep", "fsdp", None), P("fsdp", None), P("fsdp", None), P("fsdp", None))
    return jax.shard_map(
        local,
        mesh=mesh,
        in_specs=placed,
        out_specs=(P("fsdp", None), P("fsdp", None), P("fsdp", None), P(None, "fsdp")),
        check_vma=False,
    )
```

profile of v0, /device:TPU:1, one launch (start us, length us, event | category | flops | bytes accessed | tf_op | source)
XLA Modules:
  0.0 226.8 jit_solution(11922680237035600617)
XLA Ops:
  7.2 0.0 copy-start.1
  7.2 0.0 copy-start
  7.2 0.0 all-reduce.2.cloned.1.call-start
  7.2 1.8 convert_bitcast_fusion
  9.1 0.0 all-reduce.2.cloned.1.call-update
  9.1 189.4 %all-reduce.2.cloned.1.call-done = bf16[8,16384]{1,0:T(8,128)(2,1)} async-done(((bf16[8,16384]{1,0:T(8,128)(2,1)}), bf16[8,16384]{1,0:T(8,128)(2,1)}) %all-reduce.2.cloned.1.call-update) | async-done | bytes 262160 | tf_op jit(solution)/shard_map/psum | solution.py:35
  198.5 0.0 copy-done.1
  198.5 0.0 copy-done
  198.5 2.5 %fusion.3 = (bf16[8,16384]{1,0:T(8,128)(2,1)S(1)}, f32[8,16384]{1,0:T(8,128)}, f32[8,16384]{1,0:T(8,128)}, f32[8,16384]{1,0:T(8,128)}) fusion(f32[8,16384]{1,0:T(8,128)S(1)} %copy-done, bf16[8,16384]{1,0:T(8,128)(2,1)} %all-reduce.2.cloned.1.call-done, f32[8,16384]{1,0:T(8,128)S(1)} %copy-done.1, f32[8,16384]{1,0:T(8,128)} %param.7), kind=kLoop, calls=%fused_computation.8 | loop fusion | flops 2359296 | bytes 3670016 | tf_op jit(solution)/shard_map/convert_element_type | solution.py:38
  201.0 18.2 %all_to_all.19 = bf16[8,32,512]{2,0,1:T(8,128)(2,1)S(1)} all-to-all(bf16[8,32,512]{2,0,1:T(8,128)(2,1)S(1)} %bitcast.6), channel_id=1, replica_groups=mesh['rep'=16,'fsdp'=32] {'fsdp'}, dimensions={1} | all-to-all | bytes 524288 | tf_op jit(solution)/shard_map/all_to_all | solution.py:37
  219.3 0.7 copy.10
Async XLA Ops:
  7.2 191.3 %copy-start.1 = (f32[8,16384]{1,0:T(8,128)S(1)}, f32[8,16384]{1,0:T(8,128)}, u32[]{:S(2)}) copy-start(f32[8,16384]{1,0:T(8,128)} %param.6) | copy-start | bytes 1572868
  7.2 191.3 %copy-start = (f32[8,16384]{1,0:T(8,128)S(1)}, f32[8,16384]{1,0:T(8,128)}, u32[]{:S(2)}) copy-start(f32[8,16384]{1,0:T(8,128)} %param.5) | copy-start | bytes 1572868
  7.2 191.3 %all-reduce.2.cloned.1.call-start = ((), (), s32[]{:S(2)}) async-start(), calls=%async_computation.1 | async-start | bytes 524288 | tf_op jit(solution)/shard_map/psum | solution.py:35
Sparse Core Ops, SparseCore 0:
  11.5 186.9 all-reduce.1
where the time goes:
time: 229 us; the launch traced here: 227 us
  waiting for transfers between devices  189 us (83%)
  blocking collectives  18.2 us (8%)
  between operations  14 us (6%)
  other arithmetic  4.38 us (2%)
    psum x1, waiting for transfers between devices, local(): lax.psum(grad_block.astype(jnp.bfloat16), 'rep').astype(jnp.float32)  189 us
    all_to_all x1, blocking collectives, local(): lax.all_to_all(new_master.astype(jnp.bfloat16), 'fsdp', split_axis=1, con...  18.2 us
  transfers between devices with their start and end apart: 1, of which 1 were waited for; matrix products, arithmetic and copies ran while one was open for 0% of the time, Pallas kernels for 0%

commit v1 on v0

v1 whole, which is shorter than its diff:
```python
import jax
import jax.numpy as jnp
from jax import lax
from jax.experimental import pallas as pl
from jax.experimental.pallas import tpu as pltpu
from jax.sharding import Mesh
from jax.sharding import PartitionSpec as P

STEP = 10
FSDP = ("z", "y_lo")
BF16, F32 = jnp.bfloat16, jnp.float32


def adamw(mean_grad, master, moment_one, moment_two):
    new_one = 0.9 * moment_one + 0.1 * mean_grad
    new_two = 0.95 * moment_two + 0.05 * mean_grad * mean_grad
    corrected_one = new_one / (1.0 - 0.9**STEP)
    corrected_two = new_two / (1.0 - 0.95**STEP)
    new_master = master - 0.02 * (corrected_one / (jnp.sqrt(corrected_two) + 1e-08) + 0.1 * master)
    return (new_master, new_one, new_two)


def finish(core, own, their, master, moment_one, moment_two):
    rows, width = master.shape
    part = own.shape[1]
    owners = width // part // 2
    steps = 8
    each = owners // steps

    def kernel(core_ref, own_ref, their_ref, master_ref, one_ref, two_ref, new_master_ref, new_one_ref, new_two_ref):
        first = core_ref[0] == 0
        for owner in range(each):
            lines = slice(owner * rows, (owner + 1) * rows)
            mine, others = own_ref[lines, :], their_ref[lines, :]
            for place in range(2):
                mean_grad = jnp.where(first, mine, others) if place == 0 else jnp.where(first, others, mine)
                columns = slice((2 * owner + place) * part, (2 * owner + place + 1) * part)
                new_master, new_one, new_two = adamw(
                    mean_grad, master_ref[:, columns], one_ref[:, columns], two_ref[:, columns]
                )
                new_master_ref[:, columns] = new_master
                new_one_ref[:, columns] = new_one
                new_two_ref[:, columns] = new_two

    halves = pl.BlockSpec((each * rows, part), lambda i: (i, 0))
    wholes = pl.BlockSpec((rows, width // steps), lambda i: (0, i))
    return pl.pallas_call(
        kernel,
        grid=(steps,),
        in_specs=[pl.BlockSpec(memory_space=pltpu.SMEM), halves, halves, wholes, wholes, wholes],
        out_specs=[wholes] * 3,
        out_shape=[jax.ShapeDtypeStruct((rows, width), F32)] * 3,
        cost_estimate=pl.CostEstimate(
            flops=20 * rows * width, bytes_accessed=7 * 4 * rows * width, transcendentals=rows * width
        ),
        name="finish",
    )(core.reshape(1), own, their, master, moment_one, moment_two)


def local(grads, master, moment_one, moment_two):
    rows, width = master.shape
    owners = lax.axis_size(FSDP)
    cores = lax.axis_size("core")
    rings = lax.axis_size("x")
    rep_count = cores * rings * lax.axis_size("y_hi")
    part = width // owners // cores
    core = lax.axis_index("core")
    other = [(i, cores - 1 - i) for i in range(cores)]

    def half(source, which):
        blocks = source.reshape(rows, owners, cores, part).transpose(1, 2, 0, 3)
        return lax.dynamic_index_in_dim(blocks, which, 1, keepdims=False)

    theirs = lax.ppermute(half(grads[0], 1 - core).astype(BF16), "core", other)
    chip = (half(grads[0], core) + theirs.astype(F32)).astype(BF16)
    ring = lax.all_to_all(
        jnp.broadcast_to(chip[None], (rings,) + chip.shape), "x", split_axis=0, concat_axis=0, tiled=True
    )
    line = ring.astype(F32).sum(0).astype(BF16)
    far = lax.ppermute(line, "y_hi", [(0, 1), (1, 0)])
    mean_half = (line.astype(F32) + far.astype(F32)) / rep_count

    mean_other = lax.ppermute(mean_half, "core", other)
    fresh, _, _ = adamw(mean_half, half(master, core), half(moment_one, core), half(moment_two, core))
    moved = lax.all_to_all(fresh.astype(BF16), FSDP, split_axis=0, concat_axis=0, tiled=True)
    moved = moved.reshape(owners * rows, part)
    moved_other = lax.ppermute(moved, "core", other)

    new_master, new_one, new_two = finish(
        core, mean_half.reshape(owners * rows, part), mean_other.reshape(owners * rows, part),
        master, moment_one, moment_two,
    )
    rollout = jnp.where(
        core == 0, jnp.concatenate([moved, moved_other], 1), jnp.concatenate([moved_other, moved], 1)
    )
    return (new_master, new_one, new_two, rollout)


def solution(mesh):
    devices = mesh.devices.reshape(2, 4, 2, 8, 4)
    chips = Mesh(devices, ("y_hi", "x", "core", "z", "y_lo"))
    rep = ("y_hi", "x", "core")
    placed = (P(rep, FSDP, None), P(FSDP, None), P(FSDP, None), P(FSDP, None))
    return jax.shard_map(
        local,
        mesh=chips,
        in_specs=placed,
        out_specs=(P(FSDP, None), P(FSDP, None), P(FSDP, None), P(None, FSDP)),
        check_vma=False,
    )
```

time: 229 us -> 70.5 us (0.31)
  waiting for transfers between devices: 189 us -> 23.5 us
  starting transfers between devices: 0.04 us -> 31.5 us
  blocking collectives: 18.2 us -> 0 us
  between operations: 14 us -> 0.78 us
  Pallas kernels: 0 us -> 5.57 us
  local copies, waits for them, and re-layouts: 0.71 us -> 5.24 us
    psum x1 -> x0, waiting for transfers between devices: 189 us -> none  [local(): lax.psum(grad_block.astype(jnp.bfloat16), 'rep').astype(jnp.float32)]
    ppermute x0 -> x4, starting transfers between devices: none -> 18.9 us  [the longest x1 8.79 us: local(): theirs = lax.ppermute(half(grads[0], 1 - core).astype(BF16), 'core', other)]
    all_to_all x1 -> x0, blocking collectives: 18.2 us -> none  [local(): lax.all_to_all(new_master.astype(jnp.bfloat16), 'fsdp', split_axis=1, con...]
    all_to_all x0 -> x2, waiting for transfers between devices: none -> 15.3 us  [the longest x1 8.74 us: local(): lax.all_to_all(jnp.broadcast_to(chip[None], (rings,) + chip.shape), 'x',...]
    all_to_all x0 -> x2, starting transfers between devices: none -> 12.6 us  [the longest x1 9.04 us: local(): lax.all_to_all(fresh.astype(BF16), FSDP, split_axis=0, concat_axis=0, til...]
    ppermute x0 -> x4, waiting for transfers between devices: none -> 8.22 us  [the longest x1 7.25 us: local(): far = lax.ppermute(line, 'y_hi', [(0, 1), (1, 0)])]
    pallas_call x0 -> x1, Pallas kernels: none -> 5.57 us  [finish(): pl.pallas_call(kernel, grid=(steps,), in_specs=[pl.BlockSpec(memory_space...]
  transfers between devices with their start and end apart: 1 -> 6, of which waited for: 1 -> 4; matrix products, arithmetic and copies ran while one was open for 0% -> 3% of each run, Pallas kernels for 0% -> 8%
where the time goes in v1:
time: 70.5 us; the launch traced here: 69.7 us
  starting transfers between devices  31.5 us (45%)
  waiting for transfers between devices  23.5 us (33%)
  Pallas kernels  5.57 us (8%)
  local copies, waits for them, and re-layouts  5.24 us (7%)
  other arithmetic  3.15 us (4%)
  between operations  0.78 us (1%)
    all_to_all x1, starting transfers between devices, local(): lax.all_to_all(fresh.astype(BF16), FSDP, split_axis=0, concat_axis=0, til...  9.04 us
    ppermute x1, starting transfers between devices, local(): theirs = lax.ppermute(half(grads[0], 1 - core).astype(BF16), 'core', other)  8.79 us
    all_to_all x1, waiting for transfers between devices, local(): lax.all_to_all(jnp.broadcast_to(chip[None], (rings,) + chip.shape), 'x',...  8.74 us
    ppermute x1, waiting for transfers between devices, local(): far = lax.ppermute(line, 'y_hi', [(0, 1), (1, 0)])  7.25 us
    all_to_all x1, waiting for transfers between devices, local(): lax.all_to_all(fresh.astype(BF16), FSDP, split_axis=0, concat_axis=0, til...  6.53 us
    pallas_call x1, Pallas kernels, finish(): pl.pallas_call(kernel, grid=(steps,), in_specs=[pl.BlockSpec(memory_space...  5.57 us
    ppermute x1, starting transfers between devices, local(): moved_other = lax.ppermute(moved, 'core', other)  4.44 us
    all_to_all x1, starting transfers between devices, local(): lax.all_to_all(jnp.broadcast_to(chip[None], (rings,) + chip.shape), 'x',...  3.6 us
  transfers between devices with their start and end apart: 6, of which 4 were waited for; matrix products, arithmetic and copies ran while one was open for 3% of the time, Pallas kernels for 8%

profile of v1, /device:TPU:1, one launch (start us, length us, event | category | flops | bytes accessed | tf_op | source)
XLA Modules:
  0.0 69.7 jit_solution(11475851154966704584)
XLA Ops:
  0.6 1.0 %fusion.12 = bf16[32,8,256]{2,1,0:T(8,128)(2,1)S(1)} fusion(f32[8,32,2,256]{3,0,2,1:T(8,128)} %bitcast.56, s32[]{:T(128)S(6)} %select_n.19), kind=kLoop, calls=%fused_computation.20 | loop fusion | bytes 262148 | tf_op jit(solution)/shard_map/convert_element_type | solution.py:74
  1.6 8.8 %collective-permute-start = (bf16[32,8,256]{2,1,0:T(8,128)(2,1)S(1)}, bf16[32,8,256]{2,1,0:T(8,128)(2,1)S(1)}, u32[]{:S(2)}, u32[]{:S(2)}) collective-permute-start(bf16[32,8,256]{2,1,0:T(8,128)(2,1)S(1)} %fusion.12), channel_id=1, source_target_pairs={{0,32},{32,0},{1,33},{33,1},{2,34},{34,2},{3,35},{35,3},{4,36},{36... | collective-permute-start | bytes 393224 | tf_op jit(solution)/shard_map/ppermute | solution.py:74
  10.4 1.0 %collective-permute-done = bf16[32,8,256]{2,1,0:T(8,128)(2,1)S(1)} collective-permute-done((bf16[32,8,256]{2,1,0:T(8,128)(2,1)S(1)}, bf16[32,8,256]{2,1,0:T(8,128)(2,1)S(1)}, u32[]{:S(2)}, u32[]{:S(2)}) %collective-permute-start) | collective-permute-done | bytes 131104 | tf_op jit(solution)/shard_map/ppermute | solution.py:74
  11.4 1.0 %fusion = bf16[32,8,256]{2,1,0:T(8,128)(2,1)S(1)} fusion(bf16[32,8,256]{2,1,0:T(8,128)(2,1)S(1)} %collective-permute-done, f32[8,32,2,256]{3,0,2,1:T(8,128)} %bitcast.57, s32[]{:T(128)S(6)} %select_n.18), kind=kLoop, calls=%fused_computation.2 | loop fusion | flops 196608 | bytes 524292 | tf_op jit(solution)/shard_map/convert_element_type | solution.py:75
  12.3 0.8 %broadcast_in_dim.2 = bf16[4,32,8,256]{3,2,1,0:T(8,128)(2,1)} broadcast(bf16[32,8,256]{2,1,0:T(8,128)(2,1)S(1)} %fusion), dimensions={1,2,3} | broadcast | bytes 655360 | tf_op jit(solution)/shard_map/broadcast_in_dim | solution.py:77
  13.2 3.6 %all-to-all-start = ((bf16[4,32,8,256]{3,2,1,0:T(8,128)(2,1)}), bf16[4,32,8,256]{3,2,1,0:T(8,128)(2,1)S(1)}, u32[]{:S(2)}, u32[]{:S(2)}) async-start(bf16[4,32,8,256]{3,2,1,0:T(8,128)(2,1)} %broadcast_in_dim.2), calls=%async_computation | async-start | bytes 1048576 | tf_op jit(solution)/shard_map/all_to_all | solution.py:76
  16.8 0.4 reshape.38
  17.3 8.7 %all-to-all-done = bf16[4,32,8,256]{3,2,1,0:T(8,128)(2,1)S(1)} async-done(((bf16[4,32,8,256]{3,2,1,0:T(8,128)(2,1)}), bf16[4,32,8,256]{3,2,1,0:T(8,128)(2,1)S(1)}, u32[]{:S(2)}, u32[]{:S(2)}) %all-to-all-start) | async-done | bytes 524320 | tf_op jit(solution)/shard_map/all_to_all | solution.py:76
  26.0 0.1 reduce_sum.12
  26.1 2.3 %collective-permute-start.1 = (bf16[32,8,256]{2,1,0:T(8,128)(2,1)S(1)}, bf16[32,8,256]{2,1,0:T(8,128)(2,1)S(1)}, u32[]{:S(2)}, u32[]{:S(2)}) collective-permute-start(bf16[32,8,256]{2,1,0:T(8,128)(2,1)S(1)} %reduce_sum.12), channel_id=1, source_target_pairs={{0,256},{256,0},{1,257},{257,1},{2,258},{258,2},{3,259},{259,3},{4... | collective-permute-start | bytes 393224 | tf_op jit(solution)/shard_map/ppermute | solution.py:80
  28.4 0.3 constant_dynamic-slice_fusion.2
  28.7 0.4 reshape.40
  29.2 0.6 copy-done.1
  29.8 0.4 reshape.39
  30.2 0.5 constant_dynamic-slice_fusion
  30.8 7.2 %collective-permute-done.1 = bf16[32,8,256]{2,1,0:T(8,128)(2,1)S(1)} collective-permute-done((bf16[32,8,256]{2,1,0:T(8,128)(2,1)S(1)}, bf16[32,8,256]{2,1,0:T(8,128)(2,1)S(1)}, u32[]{:S(2)}, u32[]{:S(2)}) %collective-permute-start.1) | collective-permute-done | bytes 131104 | tf_op jit(solution)/shard_map/ppermute | solution.py:80
  38.0 1.3 %subtract_convert_fusion = (bf16[32,8,256]{2,1,0:T(8,128)(2,1)}, f32[256,256]{1,0:T(8,128)}, f32[32,8,256]{2,1,0:T(8,128)S(1)}) fusion(f32[8,32,1,256]{3,2,1,0:T(1,128)S(1)} %get-tuple-element.13, f32[8,32,1,256]{3,2,1,0:T(1,128)S(1)} %get-tuple-element.14, f32[8,32,1,256]{3,2,1,0:T(1,128)S(1)} %constant_dynamic-slice_fusion.2, ...), kind=kLoop, calls=%fused_computation.16 | loop fusion | flops 1310720 | bytes 1703936 | tf_op jit(solution)/shard_map/convert_element_type | solution.py:85
  39.3 9.0 %all-to-all-start.1 = ((bf16[32,8,256]{2,1,0:T(8,128)(2,1)}), bf16[32,8,256]{2,1,0:T(8,128)(2,1)S(1)}, u32[]{:S(2)}, u32[]{:S(2)}) async-start(bf16[32,8,256]{2,1,0:T(8,128)(2,1)} %get-tuple-element.10), calls=%async_computation.1 | async-start | bytes 262144 | tf_op jit(solution)/shard_map/all_to_all | solution.py:85
  48.3 3.3 %collective-permute-start.2 = (f32[32,8,256]{2,1,0:T(8,128)S(1)}, f32[32,8,256]{2,1,0:T(8,128)S(1)}, u32[]{:S(2)}, u32[]{:S(2)}) collective-permute-start(f32[32,8,256]{2,1,0:T(8,128)S(1)} %get-tuple-element.12), channel_id=1, source_target_pairs={{0,32},{32,0},{1,33},{33,1},{2,34},{34,2},{3,35},{35,3},{4,36},{36... | collective-permute-start | bytes 786440 | tf_op jit(solution)/shard_map/ppermute | solution.py:83
  51.6 6.5 %all-to-all-done.1 = bf16[32,8,256]{2,1,0:T(8,128)(2,1)S(1)} async-done(((bf16[32,8,256]{2,1,0:T(8,128)(2,1)}), bf16[32,8,256]{2,1,0:T(8,128)(2,1)S(1)}, u32[]{:S(2)}, u32[]{:S(2)}) %all-to-all-start.1) | async-done | bytes 131104 | tf_op jit(solution)/shard_map/all_to_all | solution.py:85
  58.2 4.4 %collective-permute-start.3 = (bf16[256,256]{1,0:T(8,128)(2,1)S(1)}, bf16[256,256]{1,0:T(8,128)(2,1)S(1)}, u32[]{:S(2)}, u32[]{:S(2)}) collective-permute-start(bf16[256,256]{1,0:T(8,128)(2,1)S(1)} %bitcast.54), channel_id=1, source_target_pairs={{0,32},{32,0},{1,33},{33,1},{2,34},{34,2},{3,35},{35,3},{4,36},{36... | collective-permute-start | bytes 393224 | tf_op jit(solution)/shard_map/ppermute | solution.py:87
  62.6 0.7 copy-done.3
  63.3 5.6 %finish.1 = (f32[8,16384]{1,0:T(8,128)}, f32[8,16384]{1,0:T(8,128)}, f32[8,16384]{1,0:T(8,128)}) custom-call(s32[1]{0:T(128)} %bitcast.core_ref, f32[256,256]{1,0:T(8,128)} %get-tuple-element.11.own_ref, f32[256,256]{1,0:T(8,128)} %bitcast.58, f32[8,16384]{1,0:T(8,128)} %master_ref.1, f32[8,16384]{1,0:T(8,128)} %one_ref.1, f32[8,16384]{1,0:T(8,128)} %two_ref.1), custom_call_target="tpu_custom_call" | custom-call | flops 2621440 | bytes 3670016 | tf_op jit(solution)/shard_map/finish/pallas_call | solution.py:47
  68.9 0.8 %maximum_select_fusion = bf16[256,512]{1,0:T(8,128)(2,1)} fusion(bf16[256,256]{1,0:T(8,128)(2,1)S(1)} %collective-permute-done.3, bf16[256,256]{1,0:T(8,128)(2,1)S(1)} %bitcast.55, pred[]{:T(512)S(6)} %eq.3), kind=kLoop, calls=%fused_computation | loop fusion | flops 1179648 | bytes 524289 | tf_op jit(solution)/shard_map/jit(_where)/select_n | solution.py:93
  (8 shorter events, 0.0 us)
Async XLA Ops:
  1.6 9.8 %collective-permute-start = (bf16[32,8,256]{2,1,0:T(8,128)(2,1)S(1)}, bf16[32,8,256]{2,1,0:T(8,128)(2,1)S(1)}, u32[]{:S(2)}, u32[]{:S(2)}) collective-permute-start(bf16[32,8,256]{2,1,0:T(8,128)(2,1)S(1)} %fusion.12), channel_id=1, source_target_pairs={{0,32},{32,0},{1,33},{33,1},{2,34},{34,2},{3,35},{35,3},{4,36},{36... | collective-permute-start | bytes 393224 | tf_op jit(solution)/shard_map/ppermute | solution.py:74
  13.2 3.6 %copy-start.2 = (f32[8,16384]{1,0:T(8,128)S(1)}, f32[8,16384]{1,0:T(8,128)}, u32[]{:S(2)}) copy-start(f32[8,16384]{1,0:T(8,128)} %master_ref.1) | copy-start | bytes 1572868
  13.2 12.8 %all-to-all-start = ((bf16[4,32,8,256]{3,2,1,0:T(8,128)(2,1)}), bf16[4,32,8,256]{3,2,1,0:T(8,128)(2,1)S(1)}, u32[]{:S(2)}, u32[]{:S(2)}) async-start(bf16[4,32,8,256]{3,2,1,0:T(8,128)(2,1)} %broadcast_in_dim.2), calls=%async_computation | async-start | bytes 1048576 | tf_op jit(solution)/shard_map/all_to_all | solution.py:76
  17.2 11.5 %copy-start = (f32[8,16384]{1,0:T(8,128)S(1)}, f32[8,16384]{1,0:T(8,128)}, u32[]{:S(2)}) copy-start(f32[8,16384]{1,0:T(8,128)} %two_ref.1) | copy-start | bytes 1572868
  26.1 11.9 %collective-permute-start.1 = (bf16[32,8,256]{2,1,0:T(8,128)(2,1)S(1)}, bf16[32,8,256]{2,1,0:T(8,128)(2,1)S(1)}, u32[]{:S(2)}, u32[]{:S(2)}) collective-permute-start(bf16[32,8,256]{2,1,0:T(8,128)(2,1)S(1)} %reduce_sum.12), channel_id=1, source_target_pairs={{0,256},{256,0},{1,257},{257,1},{2,258},{258,2},{3,259},{259,3},{4... | collective-permute-start | bytes 393224 | tf_op jit(solution)/shard_map/ppermute | solution.py:80
  28.7 1.0 %copy-start.1 = (f32[8,16384]{1,0:T(8,128)S(1)}, f32[8,16384]{1,0:T(8,128)}, u32[]{:S(2)}) copy-start(f32[8,16384]{1,0:T(8,128)} %one_ref.1) | copy-start | bytes 1572868
  39.3 18.9 %all-to-all-start.1 = ((bf16[32,8,256]{2,1,0:T(8,128)(2,1)}), bf16[32,8,256]{2,1,0:T(8,128)(2,1)S(1)}, u32[]{:S(2)}, u32[]{:S(2)}) async-start(bf16[32,8,256]{2,1,0:T(8,128)(2,1)} %get-tuple-element.10), calls=%async_computation.1 | async-start | bytes 262144 | tf_op jit(solution)/shard_map/all_to_all | solution.py:85
  48.3 14.3 %collective-permute-start.2 = (f32[32,8,256]{2,1,0:T(8,128)S(1)}, f32[32,8,256]{2,1,0:T(8,128)S(1)}, u32[]{:S(2)}, u32[]{:S(2)}) collective-permute-start(f32[32,8,256]{2,1,0:T(8,128)S(1)} %get-tuple-element.12), channel_id=1, source_target_pairs={{0,32},{32,0},{1,33},{33,1},{2,34},{34,2},{3,35},{35,3},{4,36},{36... | collective-permute-start | bytes 786440 | tf_op jit(solution)/shard_map/ppermute | solution.py:83
  58.2 10.7 %collective-permute-start.3 = (bf16[256,256]{1,0:T(8,128)(2,1)S(1)}, bf16[256,256]{1,0:T(8,128)(2,1)S(1)}, u32[]{:S(2)}, u32[]{:S(2)}) collective-permute-start(bf16[256,256]{1,0:T(8,128)(2,1)S(1)} %bitcast.54), channel_id=1, source_target_pairs={{0,32},{32,0},{1,33},{33,1},{2,34},{34,2},{3,35},{35,3},{4,36},{36... | collective-permute-start | bytes 393224 | tf_op jit(solution)/shard_map/ppermute | solution.py:87
  62.6 0.7 %copy-start.3 = (f32[32,8,256]{2,1,0:T(8,128)}, f32[32,8,256]{2,1,0:T(8,128)S(1)}, u32[]{:S(2)}) copy-start(f32[32,8,256]{2,1,0:T(8,128)S(1)} %collective-permute-done.2) | copy-start | bytes 786436

commit v2 on v1

v2 whole, which is shorter than its diff:
```python
import jax
import jax.numpy as jnp
from jax import lax
from jax.experimental import pallas as pl
from jax.experimental.pallas import tpu as pltpu
from jax.sharding import Mesh
from jax.sharding import PartitionSpec as P

STEP = 10
FSDP = ("z", "y_lo")
BF16, F32 = jnp.bfloat16, jnp.float32


def adamw(mean_grad, master, moment_one, moment_two):
    new_one = 0.9 * moment_one + 0.1 * mean_grad
    new_two = 0.95 * moment_two + 0.05 * mean_grad * mean_grad
    corrected_one = new_one * (1.0 / (1.0 - 0.9**STEP))
    corrected_two = new_two * (1.0 / (1.0 - 0.95**STEP))
    new_master = master - 0.02 * (corrected_one / (jnp.sqrt(corrected_two) + 1e-08) + 0.1 * master)
    return (new_master, new_one, new_two)


def finish(mean_grad, master, moment_one, moment_two):
    rows, width = master.shape
    cores, _, part = mean_grad.shape
    owners = width // part // cores
    steps = 4
    each = owners // steps

    def kernel(mean_ref, master_ref, one_ref, two_ref, new_master_ref, new_one_ref, new_two_ref):
        for owner in range(each):
            for place in range(cores):
                columns = slice((cores * owner + place) * part, (cores * owner + place + 1) * part)
                new_master, new_one, new_two = adamw(
                    mean_ref[place, owner * rows : (owner + 1) * rows, :],
                    master_ref[:, columns],
                    one_ref[:, columns],
                    two_ref[:, columns],
                )
                new_master_ref[:, columns] = new_master
                new_one_ref[:, columns] = new_one
                new_two_ref[:, columns] = new_two

    wholes = pl.BlockSpec((rows, width // steps), lambda i: (0, i))
    return pl.pallas_call(
        kernel,
        grid=(steps,),
        in_specs=[pl.BlockSpec((cores, each * rows, part), lambda i: (0, i, 0)), wholes, wholes, wholes],
        out_specs=[wholes] * 3,
        out_shape=[jax.ShapeDtypeStruct((rows, width), F32)] * 3,
        cost_estimate=pl.CostEstimate(
            flops=20 * rows * width, bytes_accessed=7 * 4 * rows * width, transcendentals=rows * width
        ),
        name="finish",
    )(mean_grad, master, moment_one, moment_two)


def pack(core, arrays, part):
    rows, width = arrays[0].shape
    owners = width // part // 2
    steps = 4
    each = owners // steps

    def kernel(core_ref, *refs):
        out_ref = refs[-1]
        for owner in range(each):
            start = pl.multiple_of(2 * owner * part + core_ref[0] * part, part)
            for k, ref in enumerate(refs[:-1]):
                out_ref[owner, k] = ref[:, pl.ds(start, part)]

    return pl.pallas_call(
        kernel,
        grid=(steps,),
        in_specs=[pl.BlockSpec(memory_space=pltpu.SMEM)]
        + [pl.BlockSpec((rows, width // steps), lambda i: (0, i))] * len(arrays),
        out_specs=pl.BlockSpec((each, len(arrays), rows, part), lambda i: (i, 0, 0, 0)),
        out_shape=jax.ShapeDtypeStruct((owners, len(arrays), rows, part), F32),
        cost_estimate=pl.CostEstimate(flops=0, bytes_accessed=6 * len(arrays) * rows * width, transcendentals=0),
        name="pack",
    )(core.reshape(1), *arrays)


def local(grads, master, moment_one, moment_two):
    rows, width = master.shape
    owners = lax.axis_size(FSDP)
    cores = lax.axis_size("core")
    rings = lax.axis_size("x")
    rep_count = cores * rings * lax.axis_size("y_hi")
    part = width // owners // cores
    core = lax.axis_index("core")

    chips = lax.all_gather(grads[0].astype(BF16), "core")
    chips = chips.reshape(cores, rows, owners, cores, part).transpose(0, 2, 3, 1, 4)
    chip = lax.dynamic_index_in_dim(chips, core, 2, keepdims=False).astype(F32).sum(0).astype(BF16)
    ring = lax.all_to_all(
        jnp.broadcast_to(chip[None], (rings,) + chip.shape), "x", split_axis=0, concat_axis=0, tiled=True
    )
    states = pack(core, (master, moment_one, moment_two), part)
    ring, states = lax.optimization_barrier((ring, states))
    line = ring.astype(F32).sum(0).astype(BF16)
    mean_half = lax.all_gather(line, "y_hi").astype(F32).sum(0) / rep_count

    fresh, _, _ = adamw(mean_half, states[:, 0], states[:, 1], states[:, 2])
    moved = lax.all_to_all(fresh.astype(BF16), FSDP, split_axis=0, concat_axis=0, tiled=True)
    mean_grad = lax.all_gather(mean_half.reshape(owners * rows, part), "core")
    new_master, new_one, new_two = finish(mean_grad, master, moment_one, moment_two)
    moved, new_master, new_one, new_two = lax.optimization_barrier((moved, new_master, new_one, new_two))
    rollout = lax.all_gather(moved.reshape(owners * rows, part), "core", axis=1, tiled=True)
    return (new_master, new_one, new_two, rollout)


def solution(mesh):
    devices = mesh.devices.reshape(2, 4, 2, 8, 4)
    chips = Mesh(devices, ("y_hi", "x", "core", "z", "y_lo"))
    rep = ("y_hi", "x", "core")
    placed = (P(rep, FSDP, None), P(FSDP, None), P(FSDP, None), P(FSDP, None))
    return jax.shard_map(
        local,
        mesh=chips,
        in_specs=placed,
        out_specs=(P(FSDP, None), P(FSDP, None), P(FSDP, None), P(None, FSDP)),
        check_vma=False,
    )
```

time: 70.5 us -> 59.8 us (0.85)
  blocking collectives: 0 us -> 27 us
  starting transfers between devices: 31.5 us -> 12.5 us
  waiting for transfers between devices: 23.5 us -> 8.35 us
  local copies, waits for them, and re-layouts: 5.24 us -> 1.53 us
  Pallas kernels: 5.57 us -> 7.26 us
  other arithmetic: 3.15 us -> 2.1 us
    all_gather x0 -> x4, blocking collectives: none -> 27 us  [the longest x1 10.7 us: local(): mean_half = lax.all_gather(line, 'y_hi').astype(F32).sum(0) / rep_count]
    ppermute x4 -> x0, starting transfers between devices: 18.9 us -> none  [the longest x1 8.79 us: local(): theirs = lax.ppermute(half(grads[0], 1 - core).astype(BF16), 'core', other)]
    ppermute x4 -> x0, waiting for transfers between devices: 8.22 us -> none  [the longest x1 7.25 us: local(): far = lax.ppermute(line, 'y_hi', [(0, 1), (1, 0)])]
    all_to_all x1, waiting for transfers between devices: 6.53 us -> 2.62 us  [local(): lax.all_to_all(fresh.astype(BF16), FSDP, split_axis=0, concat_axis=0, til...]
    all_to_all x1, waiting for transfers between devices: 8.74 us -> 5.74 us  [local(): lax.all_to_all(jnp.broadcast_to(chip[None], (rings,) + chip.shape), 'x',...]
    pallas_call x1 -> x2, Pallas kernels: 5.57 us -> 7.26 us  [the longest x1 3.8 us: finish(): pl.pallas_call(kernel, grid=(steps,), in_specs=[pl.BlockSpec((cores, each...]
    reshape x3 -> x0, local copies, waits for them, and re-layouts: 1.33 us -> none  [half(): blocks = source.reshape(rows, owners, cores, part).transpose(1, 2, 0, 3)]
    convert_element_type x2 -> x1, other arithmetic: 2.24 us -> 1.07 us  [local(): chips = lax.all_gather(grads[0].astype(BF16), 'core')]
  transfers between devices with their start and end apart: 6 -> 2, of which waited for: 4 -> 2; matrix products, arithmetic and copies ran while one was open for 3% -> 0% of each run, Pallas kernels for 8% -> 12%
where the time goes in v2:
time: 59.8 us; the launch traced here: 59.4 us
  blocking collectives  27 us (45%)
  starting transfers between devices  12.5 us (21%)
  waiting for transfers between devices  8.35 us (14%)
  Pallas kernels  7.26 us (12%)
  other arithmetic  2.1 us (4%)
  local copies, waits for them, and re-layouts  1.53 us (3%)
  between operations  0.68 us (1%)
    all_gather x1, blocking collectives, local(): mean_half = lax.all_gather(line, 'y_hi').astype(F32).sum(0) / rep_count  10.7 us
    all_to_all x1, starting transfers between devices, local(): lax.all_to_all(fresh.astype(BF16), FSDP, split_axis=0, concat_axis=0, til...  8.99 us
    all_gather x1, blocking collectives, local(): chips = lax.all_gather(grads[0].astype(BF16), 'core')  8.69 us
    all_to_all x1, waiting for transfers between devices, local(): lax.all_to_all(jnp.broadcast_to(chip[None], (rings,) + chip.shape), 'x',...  5.74 us
    all_gather x1, blocking collectives, local(): lax.all_gather(moved.reshape(owners * rows, part), 'core', axis=1, tiled=...  4.25 us
    pallas_call x1, Pallas kernels, finish(): pl.pallas_call(kernel, grid=(steps,), in_specs=[pl.BlockSpec((cores, each...  3.8 us
    all_to_all x1, starting transfers between devices, local(): lax.all_to_all(jnp.broadcast_to(chip[None], (rings,) + chip.shape), 'x',...  3.47 us
    pallas_call x1, Pallas kernels, pack(): pl.pallas_call(kernel, grid=(steps,), in_specs=[pl.BlockSpec(memory_space...  3.46 us
  transfers between devices with their start and end apart: 2, of which 2 were waited for; matrix products, arithmetic and copies ran while one was open for 0% of the time, Pallas kernels for 12%

profile of v2, /device:TPU:1, one launch (start us, length us, event | category | flops | bytes accessed | tf_op | source)
XLA Modules:
  0.0 59.4 jit_solution(17896593826628661492)
XLA Ops:
  0.6 1.1 %convert_element_type.14 = bf16[1,8,16384]{2,1,0:T(8,128)(2,1)S(1)} convert(f32[1,8,16384]{2,1,0:T(8,128)} %param.4) | non-fusion elementwise | flops 131072 | bytes 786432 | tf_op jit(solution)/shard_map/convert_element_type | solution.py:92
  1.7 8.7 %all_gather.16 = bf16[2,8,16384]{2,1,0:T(8,128)(2,1)S(1)} all-gather(bf16[1,8,16384]{2,1,0:T(8,128)(2,1)S(1)} %convert_element_type.14), channel_id=1, replica_groups=mesh['y_hi'=2,'x'=4,'core'=2,'z'=8,'y_lo'=4] {'core'}, dimensions={0}, use_global_device_ids=true | all-gather | bytes 786432 | tf_op jit(solution)/shard_map/all_gather | solution.py:92
  10.4 0.8 %broadcast_in_dim.2 = bf16[4,32,8,256]{3,2,1,0:T(8,128)(2,1)} broadcast(bf16[32,8,256]{2,1,0:T(8,128)(2,1)S(1)} %bitcast.45), dimensions={1,2,3} | broadcast | bytes 655360 | tf_op jit(solution)/shard_map/broadcast_in_dim | solution.py:96
  11.3 3.5 %all-to-all-start = ((bf16[4,32,8,256]{3,2,1,0:T(8,128)(2,1)}), bf16[4,32,8,256]{3,2,1,0:T(8,128)(2,1)S(1)}, u32[]{:S(2)}, u32[]{:S(2)}) async-start(bf16[4,32,8,256]{3,2,1,0:T(8,128)(2,1)} %broadcast_in_dim.2), calls=%async_computation | async-start | bytes 1048576 | tf_op jit(solution)/shard_map/all_to_all | solution.py:95
  14.7 3.5 %pack.1 = f32[32,3,8,256]{3,2,1,0:T(8,128)} custom-call(s32[1]{0:T(128)} %bitcast.2.core_ref, f32[8,16384]{1,0:T(8,128)} %master_ref.1, f32[8,16384]{1,0:T(8,128)} %one_ref.1, f32[8,16384]{1,0:T(8,128)} %two_ref.1), custom_call_target="tpu_custom_call" | custom-call | bytes 2359296 | tf_op jit(solution)/shard_map/pack/pallas_call | solution.py:71
  18.2 0.0 copy-start
  18.2 5.7 %all-to-all-done = bf16[4,32,8,256]{3,2,1,0:T(8,128)(2,1)S(1)} async-done(((bf16[4,32,8,256]{3,2,1,0:T(8,128)(2,1)}), bf16[4,32,8,256]{3,2,1,0:T(8,128)(2,1)S(1)}, u32[]{:S(2)}, u32[]{:S(2)}) %all-to-all-start) | async-done | bytes 524320 | tf_op jit(solution)/shard_map/all_to_all | solution.py:95
  23.9 0.1 reduce_sum.37
  24.0 10.7 %all-gather = bf16[64,8,256]{2,1,0:T(8,128)(2,1)S(1)} all-gather(bf16[32,8,256]{2,1,0:T(8,128)(2,1)S(1)} %reduce_sum.37), channel_id=2, replica_groups=mesh['y_hi'=2,'x'=4,'core'=2,'z'=8,'y_lo'=4] {'y_hi'}, dimensions={0}, use_global_device_ids=true | all-gather | bytes 393216 | tf_op jit(solution)/shard_map/all_gather | solution.py:101
  34.7 0.0 copy-done
  34.7 0.9 %multiply_bitcast_fusion = (f32[1,256,256]{2,1,0:T(8,128)S(1)}, bf16[32,8,256]{2,1,0:T(8,128)(2,1)}) fusion(f32[32,8,256]{2,1,0:T(8,128)S(1)} %convert_reduce_fusion, f32[32,3,8,256]{3,2,1,0:T(8,128)S(1)} %copy-done), kind=kLoop, calls=%fused_computation.16 | loop fusion | flops 1114112 | bytes 1441792 | tf_op jit(solution)/shard_map/div | solution.py:101
  35.6 9.0 %all-to-all-start.1 = ((bf16[32,8,256]{2,1,0:T(8,128)(2,1)}), bf16[32,8,256]{2,1,0:T(8,128)(2,1)S(1)}, u32[]{:S(2)}, u32[]{:S(2)}) async-start(bf16[32,8,256]{2,1,0:T(8,128)(2,1)} %get-tuple-element.23), calls=%async_computation.1 | async-start | bytes 262144 | tf_op jit(solution)/shard_map/all_to_all | solution.py:104
  44.6 3.4 %all_gather.19.mean_ref = f32[2,256,256]{2,1,0:T(8,128)} all-gather(f32[1,256,256]{2,1,0:T(8,128)S(1)} %get-tuple-element.22), channel_id=1, replica_groups=mesh['y_hi'=2,'x'=4,'core'=2,'z'=8,'y_lo'=4] {'core'}, dimensions={0}, use_global_device_ids=true | all-gather | bytes 786432 | tf_op jit(solution)/shard_map/all_gather | solution.py:105
  48.0 3.8 %finish.1 = (f32[8,16384]{1,0:T(8,128)}, f32[8,16384]{1,0:T(8,128)}, f32[8,16384]{1,0:T(8,128)}) custom-call(f32[2,256,256]{2,1,0:T(8,128)} %all_gather.19.mean_ref, f32[8,16384]{1,0:T(8,128)} %master_ref.1, f32[8,16384]{1,0:T(8,128)} %one_ref.1, f32[8,16384]{1,0:T(8,128)} %two_ref.1), custom_call_target="tpu_custom_call" | custom-call | flops 2621440 | bytes 3670016 | tf_op jit(solution)/shard_map/finish/pallas_call | solution.py:45
  51.8 2.6 %all-to-all-done.1 = bf16[32,8,256]{2,1,0:T(8,128)(2,1)S(1)} async-done(((bf16[32,8,256]{2,1,0:T(8,128)(2,1)}), bf16[32,8,256]{2,1,0:T(8,128)(2,1)S(1)}, u32[]{:S(2)}, u32[]{:S(2)}) %all-to-all-start.1) | async-done | bytes 131104 | tf_op jit(solution)/shard_map/all_to_all | solution.py:104
  54.5 4.2 %all_gather.20 = bf16[256,512]{1,0:T(8,128)(2,1)S(1)} all-gather(bf16[256,256]{1,0:T(8,128)(2,1)S(1)} %bitcast.44), channel_id=1, replica_groups=mesh['y_hi'=2,'x'=4,'core'=2,'z'=8,'y_lo'=4] {'core'}, dimensions={1}, use_global_device_ids=true | all-gather | bytes 393216 | tf_op jit(solution)/shard_map/all_gather | solution.py:108
  58.7 0.7 %copy.16 = bf16[256,512]{1,0:T(8,128)(2,1)} copy(bf16[256,512]{1,0:T(8,128)(2,1)S(1)} %all_gather.20) | data formatting | bytes 524288
  (2 shorter events, 0.1 us)
Async XLA Ops:
  11.3 12.7 %all-to-all-start = ((bf16[4,32,8,256]{3,2,1,0:T(8,128)(2,1)}), bf16[4,32,8,256]{3,2,1,0:T(8,128)(2,1)S(1)}, u32[]{:S(2)}, u32[]{:S(2)}) async-start(bf16[4,32,8,256]{3,2,1,0:T(8,128)(2,1)} %broadcast_in_dim.2), calls=%async_computation | async-start | bytes 1048576 | tf_op jit(solution)/shard_map/all_to_all | solution.py:95
  18.2 16.5 %copy-start = (f32[32,3,8,256]{3,2,1,0:T(8,128)S(1)}, f32[32,3,8,256]{3,2,1,0:T(8,128)}, u32[]{:S(2)}) copy-start(f32[32,3,8,256]{3,2,1,0:T(8,128)} %pack.1) | copy-start | bytes 2359300
  35.6 18.8 %all-to-all-start.1 = ((bf16[32,8,256]{2,1,0:T(8,128)(2,1)}), bf16[32,8,256]{2,1,0:T(8,128)(2,1)S(1)}, u32[]{:S(2)}, u32[]{:S(2)}) async-start(bf16[32,8,256]{2,1,0:T(8,128)(2,1)} %get-tuple-element.23), calls=%async_computation.1 | async-start | bytes 262144 | tf_op jit(solution)/shard_map/all_to_all | solution.py:104

commit v3 on v2

v3 whole, which is shorter than its diff:
```python
import jax
import jax.numpy as jnp
from jax import lax
from jax.experimental import pallas as pl
from jax.experimental.pallas import tpu as pltpu
from jax.sharding import Mesh
from jax.sharding import PartitionSpec as P

STEP = 10
FSDP = ("z", "y_lo")
BF16, F32 = jnp.bfloat16, jnp.float32


def adamw(mean_grad, master, moment_one, moment_two):
    new_one = 0.9 * moment_one + 0.1 * mean_grad
    new_two = 0.95 * moment_two + 0.05 * mean_grad * mean_grad
    corrected_one = new_one * (1.0 / (1.0 - 0.9**STEP))
    corrected_two = new_two * (1.0 / (1.0 - 0.95**STEP))
    new_master = master - 0.02 * (corrected_one / (jnp.sqrt(corrected_two) + 1e-08) + 0.1 * master)
    return (new_master, new_one, new_two)


VMEM = pl.BlockSpec(memory_space=pltpu.VMEM)


def combine(chips, owners):
    cores, rows, width = chips.shape
    part = width // owners // cores

    def kernel(chips_ref, sum_ref):
        core = lax.axis_index("core")
        for owner in range(0, owners, 2):
            sums = []
            for k in range(2):
                columns = pl.ds(pl.multiple_of((cores * (owner + k) + core) * part, part), part)
                sums.append(chips_ref[0, :, columns].astype(F32) + chips_ref[1, :, columns].astype(F32))
            sum_ref[owner * rows : (owner + 2) * rows, :] = jnp.concatenate(sums, 0).astype(BF16)

    return pl.pallas_call(
        kernel,
        in_specs=[VMEM],
        out_specs=VMEM,
        out_shape=jax.ShapeDtypeStruct((owners * rows, part), BF16),
        compiler_params=pltpu.CompilerParams(vmem_limit_bytes=8 * 2**20),
        cost_estimate=pl.CostEstimate(flops=rows * width, bytes_accessed=5 * rows * width, transcendentals=0),
        name="combine",
    )(chips)


def begin(lines, master, moment_one, moment_two, rep_count):
    rows, width = master.shape
    _, tall, part = lines.shape
    owners = tall // rows
    cores = width // part // owners

    def kernel(lines_ref, master_ref, one_ref, two_ref, fresh_ref, mean_ref):
        core = lax.axis_index("core")
        for owner in range(0, owners, 2):
            pair = slice(owner * rows, (owner + 2) * rows)
            mean_grad = (lines_ref[0, pair, :].astype(F32) + lines_ref[1, pair, :].astype(F32)) / rep_count
            mean_ref[pair, :] = mean_grad
            news = []
            for k in range(2):
                columns = pl.ds(pl.multiple_of((cores * (owner + k) + core) * part, part), part)
                new_master, _, _ = adamw(
                    mean_grad[k * rows : (k + 1) * rows],
                    master_ref[:, columns],
                    one_ref[:, columns],
                    two_ref[:, columns],
                )
                news.append(new_master)
            fresh_ref[pair, :] = jnp.concatenate(news, 0).astype(BF16)

    return pl.pallas_call(
        kernel,
        in_specs=[VMEM] * 4,
        out_specs=[VMEM] * 2,
        out_shape=[jax.ShapeDtypeStruct((tall, part), BF16), jax.ShapeDtypeStruct((tall, part), F32)],
        compiler_params=pltpu.CompilerParams(vmem_limit_bytes=16 * 2**20),
        cost_estimate=pl.CostEstimate(
            flops=20 * tall * part, bytes_accessed=20 * tall * part, transcendentals=tall * part
        ),
        name="begin",
    )(lines, master, moment_one, moment_two)


def finish(mean_grad, master, moment_one, moment_two):
    rows, width = master.shape
    cores, _, part = mean_grad.shape
    owners = width // part // cores
    steps = 4
    each = owners // steps

    def kernel(mean_ref, master_ref, one_ref, two_ref, *refs):
        outs, (held, sems) = refs[:3], refs[3:]
        copies = []
        for step in range(steps):
            for owner in range(step * each, (step + 1) * each):
                for place in range(cores):
                    columns = slice((cores * owner + place) * part, (cores * owner + place + 1) * part)
                    news = adamw(
                        mean_ref[place, owner * rows : (owner + 1) * rows, :],
                        master_ref[:, columns],
                        one_ref[:, columns],
                        two_ref[:, columns],
                    )
                    for k in range(3):
                        held[k, :, columns] = news[k]
            span = pl.ds(step * width // steps, width // steps)
            for k in range(3):
                copy = pltpu.make_async_copy(held.at[k, :, span], outs[k].at[:, span], sems.at[step, k])
                copy.start()
                copies.append(copy)
        for copy in copies:
            copy.wait()

    return pl.pallas_call(
        kernel,
        in_specs=[VMEM] * 4,
        out_specs=[pl.BlockSpec(memory_space=pl.ANY)] * 3,
        out_shape=[jax.ShapeDtypeStruct((rows, width), F32)] * 3,
        scratch_shapes=[pltpu.VMEM((3, rows, width), F32), pltpu.SemaphoreType.DMA((steps, 3))],
        compiler_params=pltpu.CompilerParams(vmem_limit_bytes=16 * 2**20),
        cost_estimate=pl.CostEstimate(
            flops=20 * rows * width, bytes_accessed=7 * 4 * rows * width, transcendentals=rows * width
        ),
        name="finish",
    )(mean_grad, master, moment_one, moment_two)


def local(grads, master, moment_one, moment_two):
    rows, width = master.shape
    owners = lax.axis_size(FSDP)
    cores = lax.axis_size("core")
    rep_count = cores * lax.axis_size("x") * lax.axis_size("y_hi")
    total = combine(lax.all_gather(grads[0].astype(BF16), "core"), owners)
    for pairs in ([[0, 1], [2, 3]], [[0, 3], [1, 2]]):
        total = lax.all_gather(total, "x", axis_index_groups=pairs).astype(F32).sum(0).astype(BF16)
    lines = lax.all_gather(total, "y_hi")

    fresh, mean_half = begin(lines, master, moment_one, moment_two, rep_count)
    moved = lax.all_to_all(fresh.reshape(owners, rows, -1), FSDP, split_axis=0, concat_axis=0, tiled=True)
    mean_grad = lax.all_gather(mean_half, "core")
    new_master, new_one, new_two = finish(mean_grad, master, moment_one, moment_two)
    moved, new_master, new_one, new_two = lax.optimization_barrier((moved, new_master, new_one, new_two))
    rollout = lax.all_gather(moved.reshape(fresh.shape), "core", axis=1, tiled=True)
    return (new_master, new_one, new_two, rollout)


def solution(mesh):
    devices = mesh.devices.reshape(2, 4, 2, 8, 4)
    chips = Mesh(devices, ("y_hi", "x", "core", "z", "y_lo"))
    rep = ("y_hi", "x", "core")
    placed = (P(rep, FSDP, None), P(FSDP, None), P(FSDP, None), P(FSDP, None))
    return jax.shard_map(
        local,
        mesh=chips,
        in_specs=placed,
        out_specs=(P(FSDP, None), P(FSDP, None), P(FSDP, None), P(None, FSDP)),
        check_vma=False,
    )
```

time: 59.8 us -> 57.6 us (0.963)
  blocking collectives: 27 us -> 39.9 us
  waiting for transfers between devices: 8.35 us -> 3.22 us
  Pallas kernels: 7.26 us -> 2.29 us
  starting transfers between devices: 12.5 us -> 9.36 us
  other arithmetic: 2.1 us -> 1.16 us
  local copies, waits for them, and re-layouts: 1.53 us -> 0.72 us
    all_gather x4 -> x6, blocking collectives: 27 us -> 39.9 us  [the longest x2 11.2 us: local(): lax.all_gather(total, 'x', axis_index_groups=pairs).astype(F32).sum(0)]
    all_to_all x2 -> x1, waiting for transfers between devices: 8.35 us -> 3.22 us  [local(): lax.all_to_all(fresh.reshape(owners, rows, -1), FSDP, split_axis=0, conca...]
    pallas_call x2 -> x3, Pallas kernels: 7.26 us -> 2.29 us  [the longest x1 1.34 us: finish(): pl.pallas_call(kernel, in_specs=[VMEM] * 4, out_specs=[pl.BlockSpec(memor...]
    all_to_all x2 -> x1, starting transfers between devices: 12.5 us -> 9.36 us  [local(): lax.all_to_all(fresh.reshape(owners, rows, -1), FSDP, split_axis=0, conca...]
    div x1 -> x0, other arithmetic: 0.88 us -> none  [local(): mean_half = lax.all_gather(line, 'y_hi').astype(F32).sum(0) / rep_count]
    broadcast_in_dim x1 -> x0, local copies, waits for them, and re-layouts: 0.83 us -> none  [local(): jnp.broadcast_to(chip[None], (rings,) + chip.shape)]
  transfers between devices with their start and end apart: 2 -> 1, of which waited for: 2 -> 1; matrix products, arithmetic and copies ran while one was open for 0% -> 0% of each run, Pallas kernels for 12% -> 2%
where the time goes in v3:
time: 57.6 us; the launch traced here: 57.4 us
  blocking collectives  39.9 us (69%)
  starting transfers between devices  9.36 us (16%)
  waiting for transfers between devices  3.22 us (6%)
  Pallas kernels  2.29 us (4%)
  other arithmetic  1.16 us (2%)
  local copies, waits for them, and re-layouts  0.72 us (1%)
  between operations  0.68 us (1%)
    all_gather x2, blocking collectives, local(): lax.all_gather(total, 'x', axis_index_groups=pairs).astype(F32).sum(0)  11.2 us
    all_to_all x1, starting transfers between devices, local(): lax.all_to_all(fresh.reshape(owners, rows, -1), FSDP, split_axis=0, conca...  9.36 us
    all_gather x1, blocking collectives, local(): total = combine(lax.all_gather(grads[0].astype(BF16), 'core'), owners)  8.69 us
    all_gather x1, blocking collectives, local(): lines = lax.all_gather(total, 'y_hi')  8.54 us
    all_gather x1, blocking collectives, local(): lax.all_gather(moved.reshape(fresh.shape), 'core', axis=1, tiled=True)  6.22 us
    all_gather x1, blocking collectives, local(): mean_grad = lax.all_gather(mean_half, 'core')  5.27 us
    all_to_all x1, waiting for transfers between devices, local(): lax.all_to_all(fresh.reshape(owners, rows, -1), FSDP, split_axis=0, conca...  3.22 us
    pallas_call x1, Pallas kernels, finish(): pl.pallas_call(kernel, in_specs=[VMEM] * 4, out_specs=[pl.BlockSpec(memor...  1.34 us
  transfers between devices with their start and end apart: 1, of which 1 were waited for; matrix products, arithmetic and copies ran while one was open for 0% of the time, Pallas kernels for 2%

profile of v3, /device:TPU:1, one launch (start us, length us, event | category | flops | bytes accessed | tf_op | source)
XLA Modules:
  0.0 57.4 jit_solution(8721156741596675691)
XLA Ops:
  0.6 1.1 %convert_element_type.3 = bf16[1,8,16384]{2,1,0:T(8,128)(2,1)S(1)} convert(f32[1,8,16384]{2,1,0:T(8,128)} %param.4) | non-fusion elementwise | flops 131072 | bytes 786432 | tf_op jit(solution)/shard_map/convert_element_type | solution.py:136
  1.7 8.7 %all_gather.31.chips_ref = bf16[2,8,16384]{2,1,0:T(8,128)(2,1)S(1)} all-gather(bf16[1,8,16384]{2,1,0:T(8,128)(2,1)S(1)} %convert_element_type.3), channel_id=1, replica_groups=mesh['y_hi'=2,'x'=4,'core'=2,'z'=8,'y_lo'=4] {'core'}, dimensions={0}, use_global_device_ids=true | all-gather | bytes 786432 | tf_op jit(solution)/shard_map/all_gather | solution.py:136
  10.4 5.4 %all-gather = bf16[512,256]{1,0:T(8,128)(2,1)S(1)} all-gather(bf16[256,256]{1,0:T(8,128)(2,1)S(1)} %combine.1), channel_id=2, replica_groups={{0,64},{128,192},{1,65},{129,193},{2,66},{130,194},{3,67},{131,195},{4,..., dimensions={0}, use_global_device_ids=true | all-gather | bytes 393216 | tf_op jit(solution)/shard_map/all_gather | solution.py:138
  15.8 0.0 copy-start.2
  15.9 0.0 copy-start
  15.9 0.0 copy-start.1
  15.9 5.8 %all-gather.1 = bf16[512,256]{1,0:T(8,128)(2,1)S(1)} all-gather(bf16[256,256]{1,0:T(8,128)(2,1)S(1)} %reduce_sum.24), channel_id=3, replica_groups={{0,192},{64,128},{1,193},{65,129},{2,194},{66,130},{3,195},{67,131},{4,..., dimensions={0}, use_global_device_ids=true | all-gather | bytes 393216 | tf_op jit(solution)/shard_map/all_gather | solution.py:138
  21.8 8.5 %all-gather.2 = bf16[512,256]{1,0:T(8,128)(2,1)S(1)} all-gather(bf16[256,256]{1,0:T(8,128)(2,1)S(1)} %reduce_sum.25), channel_id=4, replica_groups=mesh['y_hi'=2,'x'=4,'core'=2,'z'=8,'y_lo'=4] {'y_hi'}, dimensions={0}, use_global_device_ids=true | all-gather | bytes 393216 | tf_op jit(solution)/shard_map/all_gather | solution.py:139
  30.3 0.0 copy-done.2
  30.3 0.0 copy-done
  30.3 0.0 copy-done.1
  30.3 0.9 %begin.1 = (bf16[256,256]{1,0:T(8,128)(2,1)}, f32[256,256]{1,0:T(8,128)S(1)}) custom-call(bf16[2,256,256]{2,1,0:T(8,128)(2,1)S(1)} %bitcast.7, f32[8,16384]{1,0:T(8,128)S(1)} %copy-done, f32[8,16384]{1,0:T(8,128)S(1)} %copy-done.1, f32[8,16384]{1,0:T(8,128)S(1)} %copy-done.2), custom_call_target="tpu_custom_call" | custom-call | flops 1310720 | bytes 1310720 | tf_op jit(solution)/shard_map/begin/pallas_call | solution.py:74
  31.2 9.4 %all-to-all-start = ((bf16[32,8,256]{2,1,0:T(8,128)(2,1)}), bf16[32,8,256]{2,1,0:T(8,128)(2,1)S(1)}, u32[]{:S(2)}, u32[]{:S(2)}) async-start(bf16[32,8,256]{2,1,0:T(8,128)(2,1)} %bitcast.3), calls=%async_computation | async-start | bytes 262144 | tf_op jit(solution)/shard_map/all_to_all | solution.py:142
  40.6 5.3 %all-gather.3 = f32[512,256]{1,0:T(8,128)S(1)} all-gather(f32[256,256]{1,0:T(8,128)S(1)} %get-tuple-element.14), channel_id=5, replica_groups=mesh['y_hi'=2,'x'=4,'core'=2,'z'=8,'y_lo'=4] {'core'}, dimensions={0}, use_global_device_ids=true | all-gather | bytes 786432 | tf_op jit(solution)/shard_map/all_gather | solution.py:143
  45.9 1.3 %finish.1 = (f32[8,16384]{1,0:T(8,128)}, f32[8,16384]{1,0:T(8,128)}, f32[8,16384]{1,0:T(8,128)}) custom-call(f32[2,256,256]{2,1,0:T(8,128)S(1)} %bitcast.6, f32[8,16384]{1,0:T(8,128)S(1)} %copy-done, f32[8,16384]{1,0:T(8,128)S(1)} %copy-done.1, f32[8,16384]{1,0:T(8,128)S(1)} %copy-done.2), custom_call_target="tpu_custom_call" | custom-call | flops 2621440 | bytes 3670016 | tf_op jit(solution)/shard_map/finish/pallas_call | solution.py:117
  47.2 3.2 %all-to-all-done = bf16[32,8,256]{2,1,0:T(8,128)(2,1)S(1)} async-done(((bf16[32,8,256]{2,1,0:T(8,128)(2,1)}), bf16[32,8,256]{2,1,0:T(8,128)(2,1)S(1)}, u32[]{:S(2)}, u32[]{:S(2)}) %all-to-all-start) | async-done | bytes 131104 | tf_op jit(solution)/shard_map/all_to_all | solution.py:142
  50.4 6.2 %all_gather.40 = bf16[256,512]{1,0:T(8,128)(2,1)S(1)} all-gather(bf16[256,256]{1,0:T(8,128)(2,1)S(1)} %bitcast.10), channel_id=1, replica_groups=mesh['y_hi'=2,'x'=4,'core'=2,'z'=8,'y_lo'=4] {'core'}, dimensions={1}, use_global_device_ids=true | all-gather | bytes 393216 | tf_op jit(solution)/shard_map/all_gather | solution.py:146
  56.7 0.7 %copy.9 = bf16[256,512]{1,0:T(8,128)(2,1)} copy(bf16[256,512]{1,0:T(8,128)(2,1)S(1)} %all_gather.40) | data formatting | bytes 524288
  (3 shorter events, 0.1 us)
Async XLA Ops:
  15.8 14.5 %copy-start.2 = (f32[8,16384]{1,0:T(8,128)S(1)}, f32[8,16384]{1,0:T(8,128)}, u32[]{:S(2)}) copy-start(f32[8,16384]{1,0:T(8,128)} %two_ref.3) | copy-start | bytes 1572868
  15.9 14.5 %copy-start = (f32[8,16384]{1,0:T(8,128)S(1)}, f32[8,16384]{1,0:T(8,128)}, u32[]{:S(2)}) copy-start(f32[8,16384]{1,0:T(8,128)} %master_ref.3) | copy-start | bytes 1572868
  15.9 14.4 %copy-start.1 = (f32[8,16384]{1,0:T(8,128)S(1)}, f32[8,16384]{1,0:T(8,128)}, u32[]{:S(2)}) copy-start(f32[8,16384]{1,0:T(8,128)} %one_ref.3) | copy-start | bytes 1572868
  31.2 19.2 %all-to-all-start = ((bf16[32,8,256]{2,1,0:T(8,128)(2,1)}), bf16[32,8,256]{2,1,0:T(8,128)(2,1)S(1)}, u32[]{:S(2)}, u32[]{:S(2)}) async-start(bf16[32,8,256]{2,1,0:T(8,128)(2,1)} %bitcast.3), calls=%async_computation | async-start | bytes 262144 | tf_op jit(solution)/shard_map/all_to_all | solution.py:142

commit v4 on v3

--- a/solution.py
+++ b/solution.py
@@ -134,9 +134,11 @@
     cores = lax.axis_size("core")
     rep_count = cores * lax.axis_size("x") * lax.axis_size("y_hi")
     total = combine(lax.all_gather(grads[0].astype(BF16), "core"), owners)
-    for pairs in ([[0, 1], [2, 3]], [[0, 3], [1, 2]]):
-        total = lax.all_gather(total, "x", axis_index_groups=pairs).astype(F32).sum(0).astype(BF16)
-    lines = lax.all_gather(total, "y_hi")
+    rep = ("y_hi", "x", "core")
+    for step in zip((2, 6, 8), (8, 2, 6)):
+        pairs = [[i, i ^ step[i % 2]] for i in range(rep_count) if i < i ^ step[i % 2]]
+        lines = lax.all_gather(total, rep, axis_index_groups=pairs)
+        total = lines.astype(F32).sum(0).astype(BF16)
 
     fresh, mean_half = begin(lines, master, moment_one, moment_two, rep_count)
     moved = lax.all_to_all(fresh.reshape(owners, rows, -1), FSDP, split_axis=0, concat_axis=0, tiled=True)

time: 57.6 us -> 56.2 us (0.976)
  starting transfers between devices: 9.36 us -> 8.51 us
    all_gather x3, blocking collectives: 19.8 us -> 18.7 us  [local(): lines = lax.all_gather(total, rep, axis_index_groups=pairs)]
    all_to_all x1, starting transfers between devices: 9.36 us -> 8.51 us  [local(): lax.all_to_all(fresh.reshape(owners, rows, -1), FSDP, split_axis=0, conca...]
where the time goes in v4:
time: 56.2 us; the launch traced here: 56 us
  blocking collectives  39.8 us (71%)
  starting transfers between devices  8.51 us (15%)
  waiting for transfers between devices  2.83 us (5%)
  Pallas kernels  2.29 us (4%)
  other arithmetic  1.16 us (2%)
  local copies, waits for them, and re-layouts  0.72 us (1%)
  between operations  0.68 us (1%)
    all_gather x3, blocking collectives, local(): lines = lax.all_gather(total, rep, axis_index_groups=pairs)  18.7 us
    all_gather x1, blocking collectives, local(): total = combine(lax.all_gather(grads[0].astype(BF16), 'core'), owners)  8.69 us
    all_to_all x1, starting transfers between devices, local(): lax.all_to_all(fresh.reshape(owners, rows, -1), FSDP, split_axis=0, conca...  8.51 us
    all_gather x1, blocking collectives, local(): lax.all_gather(moved.reshape(fresh.shape), 'core', axis=1, tiled=True)  6.62 us
    all_gather x1, blocking collectives, local(): mean_grad = lax.all_gather(mean_half, 'core')  5.75 us
    all_to_all x1, waiting for transfers between devices, local(): lax.all_to_all(fresh.reshape(owners, rows, -1), FSDP, split_axis=0, conca...  2.83 us
    pallas_call x1, Pallas kernels, finish(): pl.pallas_call(kernel, in_specs=[VMEM] * 4, out_specs=[pl.BlockSpec(memor...  1.34 us
  transfers between devices with their start and end apart: 1, of which 1 were waited for; matrix products, arithmetic and copies ran while one was open for 0% of the time, Pallas kernels for 2%

profile of v4, /device:TPU:1, one launch (start us, length us, event | category | flops | bytes accessed | tf_op | source)
XLA Modules:
  0.0 56.0 jit_solution(11875471166886012205)
XLA Ops:
  0.6 1.1 %convert_element_type.3 = bf16[1,8,16384]{2,1,0:T(8,128)(2,1)S(1)} convert(f32[1,8,16384]{2,1,0:T(8,128)} %param.4) | non-fusion elementwise | flops 131072 | bytes 786432 | tf_op jit(solution)/shard_map/convert_element_type | solution.py:136
  1.7 8.7 %all_gather.31.chips_ref = bf16[2,8,16384]{2,1,0:T(8,128)(2,1)S(1)} all-gather(bf16[1,8,16384]{2,1,0:T(8,128)(2,1)S(1)} %convert_element_type.3), channel_id=1, replica_groups=mesh['y_hi'=2,'x'=4,'core'=2,'z'=8,'y_lo'=4] {'core'}, dimensions={0}, use_global_device_ids=true | all-gather | bytes 786432 | tf_op jit(solution)/shard_map/all_gather | solution.py:136
  10.4 8.4 %all-gather = bf16[512,256]{1,0:T(8,128)(2,1)S(1)} all-gather(bf16[256,256]{1,0:T(8,128)(2,1)S(1)} %combine.1), channel_id=2, replica_groups={{0,64},{32,288},{96,352},{128,192},{160,416},{224,480},{256,320},{384,4..., dimensions={0}, use_global_device_ids=true | all-gather | bytes 393216 | tf_op jit(solution)/shard_map/all_gather | solution.py:140
  18.8 0.0 copy-start.2
  18.9 0.0 copy-start
  18.9 0.0 copy-start.1
  18.9 4.6 %all-gather.1 = bf16[512,256]{1,0:T(8,128)(2,1)S(1)} all-gather(bf16[256,256]{1,0:T(8,128)(2,1)S(1)} %reduce_sum.24), channel_id=3, replica_groups={{0,192},{32,96},{64,128},{160,224},{256,448},{288,352},{320,384},{416,4..., dimensions={0}, use_global_device_ids=true | all-gather | bytes 393216 | tf_op jit(solution)/shard_map/all_gather | solution.py:140
  23.6 5.7 %all-gather.2 = bf16[512,256]{1,0:T(8,128)(2,1)S(1)} all-gather(bf16[256,256]{1,0:T(8,128)(2,1)S(1)} %reduce_sum.25), channel_id=4, replica_groups={{0,256},{32,224},{64,320},{96,160},{128,384},{192,448},{288,480},{352,4..., dimensions={0}, use_global_device_ids=true | all-gather | bytes 393216 | tf_op jit(solution)/shard_map/all_gather | solution.py:140
  29.3 0.0 copy-done.2
  29.3 0.0 copy-done
  29.3 0.0 copy-done.1
  29.3 0.9 %begin.1 = (bf16[256,256]{1,0:T(8,128)(2,1)}, f32[256,256]{1,0:T(8,128)S(1)}) custom-call(bf16[2,256,256]{2,1,0:T(8,128)(2,1)S(1)} %bitcast.7, f32[8,16384]{1,0:T(8,128)S(1)} %copy-done, f32[8,16384]{1,0:T(8,128)S(1)} %copy-done.1, f32[8,16384]{1,0:T(8,128)S(1)} %copy-done.2), custom_call_target="tpu_custom_call" | custom-call | flops 1310720 | bytes 1310720 | tf_op jit(solution)/shard_map/begin/pallas_call | solution.py:74
  30.2 8.5 %all-to-all-start = ((bf16[32,8,256]{2,1,0:T(8,128)(2,1)}), bf16[32,8,256]{2,1,0:T(8,128)(2,1)S(1)}, u32[]{:S(2)}, u32[]{:S(2)}) async-start(bf16[32,8,256]{2,1,0:T(8,128)(2,1)} %bitcast.3), calls=%async_computation | async-start | bytes 262144 | tf_op jit(solution)/shard_map/all_to_all | solution.py:144
  38.7 5.8 %all-gather.3 = f32[512,256]{1,0:T(8,128)S(1)} all-gather(f32[256,256]{1,0:T(8,128)S(1)} %get-tuple-element.14), channel_id=5, replica_groups=mesh['y_hi'=2,'x'=4,'core'=2,'z'=8,'y_lo'=4] {'core'}, dimensions={0}, use_global_device_ids=true | all-gather | bytes 786432 | tf_op jit(solution)/shard_map/all_gather | solution.py:145
  44.5 1.3 %finish.1 = (f32[8,16384]{1,0:T(8,128)}, f32[8,16384]{1,0:T(8,128)}, f32[8,16384]{1,0:T(8,128)}) custom-call(f32[2,256,256]{2,1,0:T(8,128)S(1)} %bitcast.6, f32[8,16384]{1,0:T(8,128)S(1)} %copy-done, f32[8,16384]{1,0:T(8,128)S(1)} %copy-done.1, f32[8,16384]{1,0:T(8,128)S(1)} %copy-done.2), custom_call_target="tpu_custom_call" | custom-call | flops 2621440 | bytes 3670016 | tf_op jit(solution)/shard_map/finish/pallas_call | solution.py:117
  45.8 2.8 %all-to-all-done = bf16[32,8,256]{2,1,0:T(8,128)(2,1)S(1)} async-done(((bf16[32,8,256]{2,1,0:T(8,128)(2,1)}), bf16[32,8,256]{2,1,0:T(8,128)(2,1)S(1)}, u32[]{:S(2)}, u32[]{:S(2)}) %all-to-all-start) | async-done | bytes 131104 | tf_op jit(solution)/shard_map/all_to_all | solution.py:144
  48.7 6.6 %all_gather.40 = bf16[256,512]{1,0:T(8,128)(2,1)S(1)} all-gather(bf16[256,256]{1,0:T(8,128)(2,1)S(1)} %bitcast.10), channel_id=1, replica_groups=mesh['y_hi'=2,'x'=4,'core'=2,'z'=8,'y_lo'=4] {'core'}, dimensions={1}, use_global_device_ids=true | all-gather | bytes 393216 | tf_op jit(solution)/shard_map/all_gather | solution.py:148
  55.3 0.7 %copy.9 = bf16[256,512]{1,0:T(8,128)(2,1)} copy(bf16[256,512]{1,0:T(8,128)(2,1)S(1)} %all_gather.40) | data formatting | bytes 524288
  (3 shorter events, 0.1 us)
Async XLA Ops:
  18.8 10.5 %copy-start.2 = (f32[8,16384]{1,0:T(8,128)S(1)}, f32[8,16384]{1,0:T(8,128)}, u32[]{:S(2)}) copy-start(f32[8,16384]{1,0:T(8,128)} %two_ref.3) | copy-start | bytes 1572868
  18.9 10.4 %copy-start = (f32[8,16384]{1,0:T(8,128)S(1)}, f32[8,16384]{1,0:T(8,128)}, u32[]{:S(2)}) copy-start(f32[8,16384]{1,0:T(8,128)} %master_ref.3) | copy-start | bytes 1572868
  18.9 10.4 %copy-start.1 = (f32[8,16384]{1,0:T(8,128)S(1)}, f32[8,16384]{1,0:T(8,128)}, u32[]{:S(2)}) copy-start(f32[8,16384]{1,0:T(8,128)} %one_ref.3) | copy-start | bytes 1572868
  30.2 18.4 %all-to-all-start = ((bf16[32,8,256]{2,1,0:T(8,128)(2,1)}), bf16[32,8,256]{2,1,0:T(8,128)(2,1)S(1)}, u32[]{:S(2)}, u32[]{:S(2)}) async-start(bf16[32,8,256]{2,1,0:T(8,128)(2,1)} %bitcast.3), calls=%async_computation | async-start | bytes 262144 | tf_op jit(solution)/shard_map/all_to_all | solution.py:144

commit v5 on v4

--- a/solution.py
+++ b/solution.py
@@ -21,6 +21,15 @@
 
 
 VMEM = pl.BlockSpec(memory_space=pltpu.VMEM)
+REP = ("y_hi", "x", "core")
+
+
+def half_of(place):
+    return (place + place // 2 + place // 8) % 2
+
+
+def own_half():
+    return (lax.axis_index("core") + lax.axis_index("x") + lax.axis_index("y_hi")) % 2
 
 
 def combine(chips, owners):
@@ -28,11 +37,11 @@
     part = width // owners // cores
 
     def kernel(chips_ref, sum_ref):
-        core = lax.axis_index("core")
+        half = own_half()
         for owner in range(0, owners, 2):
             sums = []
             for k in range(2):
-                columns = pl.ds(pl.multiple_of((cores * (owner + k) + core) * part, part), part)
+                columns = pl.ds(pl.multiple_of((cores * (owner + k) + half) * part, part), part)
                 sums.append(chips_ref[0, :, columns].astype(F32) + chips_ref[1, :, columns].astype(F32))
             sum_ref[owner * rows : (owner + 2) * rows, :] = jnp.concatenate(sums, 0).astype(BF16)
 
@@ -54,14 +63,14 @@
     cores = width // part // owners
 
     def kernel(lines_ref, master_ref, one_ref, two_ref, fresh_ref, mean_ref):
-        core = lax.axis_index("core")
+        half = own_half()
         for owner in range(0, owners, 2):
             pair = slice(owner * rows, (owner + 2) * rows)
             mean_grad = (lines_ref[0, pair, :].astype(F32) + lines_ref[1, pair, :].astype(F32)) / rep_count
             mean_ref[pair, :] = mean_grad
             news = []
             for k in range(2):
-                columns = pl.ds(pl.multiple_of((cores * (owner + k) + core) * part, part), part)
+                columns = pl.ds(pl.multiple_of((cores * (owner + k) + half) * part, part), part)
                 new_master, _, _ = adamw(
                     mean_grad[k * rows : (k + 1) * rows],
                     master_ref[:, columns],
@@ -134,18 +143,18 @@
     cores = lax.axis_size("core")
     rep_count = cores * lax.axis_size("x") * lax.axis_size("y_hi")
     total = combine(lax.all_gather(grads[0].astype(BF16), "core"), owners)
-    rep = ("y_hi", "x", "core")
-    for step in zip((2, 6, 8), (8, 2, 6)):
-        pairs = [[i, i ^ step[i % 2]] for i in range(rep_count) if i < i ^ step[i % 2]]
-        lines = lax.all_gather(total, rep, axis_index_groups=pairs)
+    for step in zip((3, 7, 9), (9, 3, 7)):
+        pairs = [[i, i ^ step[half_of(i)]] for i in range(rep_count) if i < i ^ step[half_of(i)]]
+        lines = lax.all_gather(total, REP, axis_index_groups=pairs)
         total = lines.astype(F32).sum(0).astype(BF16)
 
     fresh, mean_half = begin(lines, master, moment_one, moment_two, rep_count)
     moved = lax.all_to_all(fresh.reshape(owners, rows, -1), FSDP, split_axis=0, concat_axis=0, tiled=True)
-    mean_grad = lax.all_gather(mean_half, "core")
+    chips = [[i + half_of(i), i + 1 - half_of(i)] for i in range(0, rep_count, 2)]
+    mean_grad = lax.all_gather(mean_half, REP, axis_index_groups=chips)
     new_master, new_one, new_two = finish(mean_grad, master, moment_one, moment_two)
     moved, new_master, new_one, new_two = lax.optimization_barrier((moved, new_master, new_one, new_two))
-    rollout = lax.all_gather(moved.reshape(fresh.shape), "core", axis=1, tiled=True)
+    rollout = lax.all_gather(moved.reshape(fresh.shape), REP, axis=1, tiled=True, axis_index_groups=chips)
     return (new_master, new_one, new_two, rollout)
 
 

time: 56.2 us -> 54.5 us (0.970)
  blocking collectives: 39.8 us -> 35 us
  waiting for transfers between devices: 2.83 us -> 6.07 us
    all_gather x5, blocking collectives: 31.1 us -> 26.3 us  [the longest x3 20.5 us: local(): lines = lax.all_gather(total, REP, axis_index_groups=pairs)]
    all_to_all x1, waiting for transfers between devices: 2.83 us -> 6.07 us  [local(): lax.all_to_all(fresh.reshape(owners, rows, -1), FSDP, split_axis=0, conca...]
where the time goes in v5:
time: 54.5 us; the launch traced here: 54.3 us
  blocking collectives  35 us (64%)
  starting transfers between devices  8.37 us (15%)
  waiting for transfers between devices  6.07 us (11%)
  Pallas kernels  2.3 us (4%)
  other arithmetic  1.16 us (2%)
  local copies, waits for them, and re-layouts  0.72 us (1%)
  between operations  0.68 us (1%)
    all_gather x3, blocking collectives, local(): lines = lax.all_gather(total, REP, axis_index_groups=pairs)  20.5 us
    all_gather x1, blocking collectives, local(): total = combine(lax.all_gather(grads[0].astype(BF16), 'core'), owners)  8.69 us
    all_to_all x1, starting transfers between devices, local(): lax.all_to_all(fresh.reshape(owners, rows, -1), FSDP, split_axis=0, conca...  8.37 us
    all_to_all x1, waiting for transfers between devices, local(): lax.all_to_all(fresh.reshape(owners, rows, -1), FSDP, split_axis=0, conca...  6.07 us
    all_gather x1, blocking collectives, local(): lax.all_gather(moved.reshape(fresh.shape), REP, axis=1, tiled=True, axis_...  3.38 us
    all_gather x1, blocking collectives, local(): mean_grad = lax.all_gather(mean_half, REP, axis_index_groups=chips)  2.42 us
    pallas_call x1, Pallas kernels, finish(): pl.pallas_call(kernel, in_specs=[VMEM] * 4, out_specs=[pl.BlockSpec(memor...  1.34 us
  transfers between devices with their start and end apart: 1, of which 1 were waited for; matrix products, arithmetic and copies ran while one was open for 0% of the time, Pallas kernels for 2%

profile of v5, /device:TPU:1, one launch (start us, length us, event | category | flops | bytes accessed | tf_op | source)
XLA Modules:
  0.0 54.3 jit_solution(12526168704832912052)
XLA Ops:
  0.6 1.1 %convert_element_type.3 = bf16[1,8,16384]{2,1,0:T(8,128)(2,1)S(1)} convert(f32[1,8,16384]{2,1,0:T(8,128)} %param.4) | non-fusion elementwise | flops 131072 | bytes 786432 | tf_op jit(solution)/shard_map/convert_element_type | solution.py:145
  1.7 8.7 %all_gather.31.chips_ref = bf16[2,8,16384]{2,1,0:T(8,128)(2,1)S(1)} all-gather(bf16[1,8,16384]{2,1,0:T(8,128)(2,1)S(1)} %convert_element_type.3), channel_id=1, replica_groups=mesh['y_hi'=2,'x'=4,'core'=2,'z'=8,'y_lo'=4] {'core'}, dimensions={0}, use_global_device_ids=true | all-gather | bytes 786432 | tf_op jit(solution)/shard_map/all_gather | solution.py:145
  10.4 9.0 %all-gather = bf16[512,256]{1,0:T(8,128)(2,1)S(1)} all-gather(bf16[256,256]{1,0:T(8,128)(2,1)S(1)} %combine.1), channel_id=2, replica_groups={{0,96},{32,256},{64,352},{128,224},{160,384},{192,480},{288,320},{416,4..., dimensions={0}, use_global_device_ids=true | all-gather | bytes 393216 | tf_op jit(solution)/shard_map/all_gather | solution.py:148
  19.4 0.0 copy-start.2
  19.5 0.0 copy-start
  19.5 0.0 copy-start.1
  19.5 5.2 %all-gather.1 = bf16[512,256]{1,0:T(8,128)(2,1)S(1)} all-gather(bf16[256,256]{1,0:T(8,128)(2,1)S(1)} %reduce_sum.24), channel_id=3, replica_groups={{0,224},{32,64},{96,128},{160,192},{256,352},{288,448},{320,416},{384,4..., dimensions={0}, use_global_device_ids=true | all-gather | bytes 393216 | tf_op jit(solution)/shard_map/all_gather | solution.py:148
  24.7 6.3 %all-gather.2 = bf16[512,256]{1,0:T(8,128)(2,1)S(1)} all-gather(bf16[256,256]{1,0:T(8,128)(2,1)S(1)} %reduce_sum.25), channel_id=4, replica_groups={{0,288},{32,192},{64,160},{96,320},{128,416},{224,448},{256,480},{352,3..., dimensions={0}, use_global_device_ids=true | all-gather | bytes 393216 | tf_op jit(solution)/shard_map/all_gather | solution.py:148
  31.0 0.0 copy-done.2
  31.0 0.0 copy-done
  31.0 0.0 copy-done.1
  31.0 0.9 %begin.1 = (bf16[256,256]{1,0:T(8,128)(2,1)}, f32[256,256]{1,0:T(8,128)S(1)}) custom-call(bf16[2,256,256]{2,1,0:T(8,128)(2,1)S(1)} %bitcast.7, f32[8,16384]{1,0:T(8,128)S(1)} %copy-done, f32[8,16384]{1,0:T(8,128)S(1)} %copy-done.1, f32[8,16384]{1,0:T(8,128)S(1)} %copy-done.2), custom_call_target="tpu_custom_call" | custom-call | flops 1310720 | bytes 1310720 | tf_op jit(solution)/shard_map/begin/pallas_call | solution.py:83
  32.0 8.4 %all-to-all-start = ((bf16[32,8,256]{2,1,0:T(8,128)(2,1)}), bf16[32,8,256]{2,1,0:T(8,128)(2,1)S(1)}, u32[]{:S(2)}, u32[]{:S(2)}) async-start(bf16[32,8,256]{2,1,0:T(8,128)(2,1)} %bitcast.3), calls=%async_computation | async-start | bytes 262144 | tf_op jit(solution)/shard_map/all_to_all | solution.py:152
  40.3 2.4 %all-gather.3 = f32[512,256]{1,0:T(8,128)S(1)} all-gather(f32[256,256]{1,0:T(8,128)S(1)} %get-tuple-element.14), channel_id=5, replica_groups={{0,32},{96,64},{128,160},{224,192},{288,256},{320,352},{416,384},{448,4..., dimensions={0}, use_global_device_ids=true | all-gather | bytes 786432 | tf_op jit(solution)/shard_map/all_gather | solution.py:154
  42.8 1.3 %finish.1 = (f32[8,16384]{1,0:T(8,128)}, f32[8,16384]{1,0:T(8,128)}, f32[8,16384]{1,0:T(8,128)}) custom-call(f32[2,256,256]{2,1,0:T(8,128)S(1)} %bitcast.6, f32[8,16384]{1,0:T(8,128)S(1)} %copy-done, f32[8,16384]{1,0:T(8,128)S(1)} %copy-done.1, f32[8,16384]{1,0:T(8,128)S(1)} %copy-done.2), custom_call_target="tpu_custom_call" | custom-call | flops 2621440 | bytes 3670016 | tf_op jit(solution)/shard_map/finish/pallas_call | solution.py:126
  44.1 6.1 %all-to-all-done = bf16[32,8,256]{2,1,0:T(8,128)(2,1)S(1)} async-done(((bf16[32,8,256]{2,1,0:T(8,128)(2,1)}), bf16[32,8,256]{2,1,0:T(8,128)(2,1)S(1)}, u32[]{:S(2)}, u32[]{:S(2)}) %all-to-all-start) | async-done | bytes 131104 | tf_op jit(solution)/shard_map/all_to_all | solution.py:152
  50.2 3.4 %all_gather.40 = bf16[256,512]{1,0:T(8,128)(2,1)S(1)} all-gather(bf16[256,256]{1,0:T(8,128)(2,1)S(1)} %bitcast.10), channel_id=1, replica_groups={{0,32},{96,64},{128,160},{224,192},{288,256},{320,352},{416,384},{448,4..., dimensions={1}, use_global_device_ids=true | all-gather | bytes 393216 | tf_op jit(solution)/shard_map/all_gather | solution.py:157
  53.6 0.7 %copy.9 = bf16[256,512]{1,0:T(8,128)(2,1)} copy(bf16[256,512]{1,0:T(8,128)(2,1)S(1)} %all_gather.40) | data formatting | bytes 524288
  (3 shorter events, 0.1 us)
Async XLA Ops:
  19.4 11.6 %copy-start.2 = (f32[8,16384]{1,0:T(8,128)S(1)}, f32[8,16384]{1,0:T(8,128)}, u32[]{:S(2)}) copy-start(f32[8,16384]{1,0:T(8,128)} %two_ref.3) | copy-start | bytes 1572868
  19.5 11.6 %copy-start = (f32[8,16384]{1,0:T(8,128)S(1)}, f32[8,16384]{1,0:T(8,128)}, u32[]{:S(2)}) copy-start(f32[8,16384]{1,0:T(8,128)} %master_ref.3) | copy-start | bytes 1572868
  19.5 11.6 %copy-start.1 = (f32[8,16384]{1,0:T(8,128)S(1)}, f32[8,16384]{1,0:T(8,128)}, u32[]{:S(2)}) copy-start(f32[8,16384]{1,0:T(8,128)} %one_ref.3) | copy-start | bytes 1572868
  32.0 18.2 %all-to-all-start = ((bf16[32,8,256]{2,1,0:T(8,128)(2,1)}), bf16[32,8,256]{2,1,0:T(8,128)(2,1)S(1)}, u32[]{:S(2)}, u32[]{:S(2)}) async-start(bf16[32,8,256]{2,1,0:T(8,128)(2,1)} %bitcast.3), calls=%async_computation | async-start | bytes 262144 | tf_op jit(solution)/shard_map/all_to_all | solution.py:152

commit v6 on v0

v6 whole, which is shorter than its diff:
```python
import jax
import jax.numpy as jnp
from jax import lax
from jax.sharding import Mesh
from jax.sharding import PartitionSpec as P

STEP = 10
FSDP = ("z", "y_lo")
BF16, F32 = jnp.bfloat16, jnp.float32
REP = ("y_hi", "x", "core")


def half_of(place):
    return (place + place // 2 + place // 8) % 2


def adamw(mean_grad, master, moment_one, moment_two):
    new_one = 0.9 * moment_one + 0.1 * mean_grad
    new_two = 0.95 * moment_two + 0.05 * mean_grad * mean_grad
    corrected_one = new_one * (1.0 / (1.0 - 0.9**STEP))
    corrected_two = new_two * (1.0 / (1.0 - 0.95**STEP))
    new_master = master - 0.02 * (corrected_one / (jnp.sqrt(corrected_two) + 1e-08) + 0.1 * master)
    return (new_master, new_one, new_two)


def local(grads, master, moment_one, moment_two):
    rows, width = master.shape
    owners = lax.axis_size(FSDP)
    rep_count = lax.axis_size(REP)
    piece = width // owners
    part = piece // 2
    first = half_of(lax.axis_index(REP)) == 0

    def blocks(source):
        return source.reshape(source.shape[:-1] + (owners, piece))

    def half(source):
        return jnp.where(first, source[..., :part], source[..., part:])

    chips = blocks(lax.all_gather(grads[0].astype(BF16), "core"))
    total = half(chips).astype(F32).sum(0).astype(BF16).transpose(1, 0, 2)
    for step in zip((3, 7, 9), (9, 3, 7)):
        pairs = [[i, i ^ step[half_of(i)]] for i in range(rep_count) if i < i ^ step[half_of(i)]]
        lines = lax.all_gather(total, REP, axis_index_groups=pairs)
        total = lines.astype(F32).sum(0).astype(BF16)
    mean_half = lines.astype(F32).sum(0) / rep_count

    masters, firsts, seconds = blocks(master), blocks(moment_one), blocks(moment_two)
    fresh, _, _ = adamw(mean_half.transpose(1, 0, 2), half(masters), half(firsts), half(seconds))
    moved = lax.all_to_all(fresh.astype(BF16).transpose(1, 0, 2), FSDP, split_axis=0, concat_axis=0, tiled=True)
    chips = [[i + half_of(i), i + 1 - half_of(i)] for i in range(0, rep_count, 2)]
    mean_grad = lax.all_gather(mean_half, REP, axis_index_groups=chips).transpose(0, 2, 1, 3)
    mean_grad = jnp.concatenate([mean_grad[0], mean_grad[1]], -1)
    news = adamw(mean_grad, masters, firsts, seconds)
    new_master, new_one, new_two = (new.reshape(rows, width) for new in news)
    moved, new_master, new_one, new_two = lax.optimization_barrier((moved, new_master, new_one, new_two))
    rollout = lax.all_gather(moved.reshape(owners * rows, part), REP, axis=1, tiled=True, axis_index_groups=chips)
    return (new_master, new_one, new_two, rollout)


def solution(mesh):
    devices = mesh.devices.reshape(2, 4, 2, 8, 4)
    chips = Mesh(devices, ("y_hi", "x", "core", "z", "y_lo"))
    rep = ("y_hi", "x", "core")
    placed = (P(rep, FSDP, None), P(FSDP, None), P(FSDP, None), P(FSDP, None))
    return jax.shard_map(
        local,
        mesh=chips,
        in_specs=placed,
        out_specs=(P(FSDP, None), P(FSDP, None), P(FSDP, None), P(None, FSDP)),
        check_vma=False,
    )
```

time: 229 us -> 54.8 us (0.24)
  waiting for transfers between devices: 189 us -> 5.85 us
  blocking collectives: 18.2 us -> 35.1 us
  between operations: 14 us -> 0.76 us
  starting transfers between devices: 0.04 us -> 8.38 us
    psum x1 -> x0, waiting for transfers between devices: 189 us -> none  [local(): lax.psum(grad_block.astype(jnp.bfloat16), 'rep').astype(jnp.float32)]
    all_gather x0 -> x6, blocking collectives: none -> 35.1 us  [the longest x3 20.6 us: local(): lines = lax.all_gather(total, REP, axis_index_groups=pairs)]
    all_to_all x1 -> x0, blocking collectives: 18.2 us -> none  [local(): lax.all_to_all(new_master.astype(jnp.bfloat16), 'fsdp', split_axis=1, con...]
    all_to_all x0 -> x1, starting transfers between devices: none -> 8.38 us  [local(): lax.all_to_all(fresh.astype(BF16).transpose(1, 0, 2), FSDP, split_axis=0,...]
    all_to_all x0 -> x1, waiting for transfers between devices: none -> 5.85 us  [local(): lax.all_to_all(fresh.astype(BF16).transpose(1, 0, 2), FSDP, split_axis=0,...]
    convert_element_type x2 -> x1, other arithmetic: 4.38 us -> 1.07 us  [local(): chips = blocks(lax.all_gather(grads[0].astype(BF16), 'core'))]
  transfers between devices with their start and end apart: 1 -> 1, of which waited for: 1 -> 1; matrix products, arithmetic and copies ran while one was open for 0% -> 3% of each run, Pallas kernels for 0% -> 0%
where the time goes in v6:
time: 54.8 us; the launch traced here: 54.5 us
  blocking collectives  35.1 us (64%)
  starting transfers between devices  8.38 us (15%)
  waiting for transfers between devices  5.85 us (11%)
  other arithmetic  3.7 us (7%)
  between operations  0.76 us (1%)
  local copies, waits for them, and re-layouts  0.75 us (1%)
    all_gather x3, blocking collectives, local(): lines = lax.all_gather(total, REP, axis_index_groups=pairs)  20.6 us
    all_gather x1, blocking collectives, local(): chips = blocks(lax.all_gather(grads[0].astype(BF16), 'core'))  8.69 us
    all_to_all x1, starting transfers between devices, local(): lax.all_to_all(fresh.astype(BF16).transpose(1, 0, 2), FSDP, split_axis=0,...  8.38 us
    all_to_all x1, waiting for transfers between devices, local(): lax.all_to_all(fresh.astype(BF16).transpose(1, 0, 2), FSDP, split_axis=0,...  5.85 us
    all_gather x1, blocking collectives, local(): lax.all_gather(moved.reshape(owners * rows, part), REP, axis=1, tiled=Tru...  3.39 us
    all_gather x1, blocking collectives, local(): lax.all_gather(mean_half, REP, axis_index_groups=chips)  2.42 us
    sub x1, other arithmetic, adamw(): master - 0.02 * (corrected_one / (jnp.sqrt(corrected_two) + 1e-08) + 0.1...  1.43 us
  transfers between devices with their start and end apart: 1, of which 1 were waited for; matrix products, arithmetic and copies ran while one was open for 3% of the time, Pallas kernels for 0%

profile of v6, /device:TPU:1, one launch (start us, length us, event | category | flops | bytes accessed | tf_op | source)
XLA Modules:
  0.0 54.5 jit_solution(2321921189415340225)
XLA Ops:
  0.7 1.1 %convert_element_type.7 = bf16[1,8,16384]{2,1,0:T(8,128)(2,1)S(1)} convert(f32[1,8,16384]{2,1,0:T(8,128)} %param.4) | non-fusion elementwise | flops 131072 | bytes 786432 | tf_op jit(solution)/shard_map/convert_element_type | solution.py:40
  1.7 8.7 %all_gather.29 = bf16[2,8,16384]{2,1,0:T(8,128)(2,1)S(1)} all-gather(bf16[1,8,16384]{2,1,0:T(8,128)(2,1)S(1)} %convert_element_type.7), channel_id=1, replica_groups=mesh['y_hi'=2,'x'=4,'core'=2,'z'=8,'y_lo'=4] {'core'}, dimensions={0}, use_global_device_ids=true | all-gather | bytes 786432 | tf_op jit(solution)/shard_map/all_gather | solution.py:40
  10.4 0.1 fusion.8
  10.5 9.0 %all-gather = bf16[64,8,256]{2,1,0:T(8,128)(2,1)S(1)} all-gather(bf16[32,8,256]{2,1,0:T(8,128)(2,1)S(1)} %bitcast.42), channel_id=2, replica_groups={{0,96},{32,256},{64,352},{128,224},{160,384},{192,480},{288,320},{416,4..., dimensions={0}, use_global_device_ids=true | all-gather | bytes 393216 | tf_op jit(solution)/shard_map/all_gather | solution.py:44
  19.5 0.0 copy-start.2
  19.6 5.2 %all-gather.1 = bf16[64,8,256]{2,1,0:T(8,128)(2,1)S(1)} all-gather(bf16[32,8,256]{2,1,0:T(8,128)(2,1)S(1)} %reduce_sum.46), channel_id=3, replica_groups={{0,224},{32,64},{96,128},{160,192},{256,352},{288,448},{320,416},{384,4..., dimensions={0}, use_global_device_ids=true | all-gather | bytes 393216 | tf_op jit(solution)/shard_map/all_gather | solution.py:44
  24.8 0.0 copy-start.1
  24.8 0.0 copy-start
  24.8 6.4 %all-gather.2 = bf16[64,8,256]{2,1,0:T(8,128)(2,1)S(1)} all-gather(bf16[32,8,256]{2,1,0:T(8,128)(2,1)S(1)} %reduce_sum.47), channel_id=4, replica_groups={{0,288},{32,192},{64,160},{96,320},{128,416},{224,448},{256,480},{352,3..., dimensions={0}, use_global_device_ids=true | all-gather | bytes 393216 | tf_op jit(solution)/shard_map/all_gather | solution.py:44
  31.3 0.0 copy-done.2
  31.3 0.0 copy-done.1
  31.3 0.0 copy-done
  31.3 0.9 %fusion.12 = bf16[32,8,256]{2,1,0:T(8,128)(2,1)} fusion(f32[32,8,256]{2,1,0:T(8,128)S(1)} %convert_reduce_fusion, f32[8,32,512]{2,0,1:T(8,128)S(1)} %bitcast.34, f32[8,32,512]{2,0,1:T(8,128)S(1)} %bitcast.33, f32[8,32,512]{2,0,1:T(8,128)S(1)} %bitcast.32, pred[]{:T(512)S(6)} %eq.5), kind=kLoop, calls=%fused_computation.25 | loop fusion | flops 1310720 | bytes 1966081 | tf_op jit(solution)/shard_map/transpose | solution.py:50
  32.2 8.4 %all-to-all-start = ((bf16[32,8,256]{2,1,0:T(8,128)(2,1)}), bf16[32,8,256]{2,1,0:T(8,128)(2,1)S(1)}, u32[]{:S(2)}, u32[]{:S(2)}) async-start(bf16[32,8,256]{2,1,0:T(8,128)(2,1)} %fusion.12), calls=%async_computation | async-start | bytes 262144 | tf_op jit(solution)/shard_map/all_to_all | solution.py:50
  40.6 2.4 %all-gather.3 = f32[64,8,256]{2,1,0:T(8,128)S(1)} all-gather(f32[32,8,256]{2,1,0:T(8,128)S(1)} %broadcast_multiply_fusion), channel_id=5, replica_groups={{0,32},{96,64},{128,160},{224,192},{288,256},{320,352},{416,384},{448,4..., dimensions={0}, use_global_device_ids=true | all-gather | bytes 786432 | tf_op jit(solution)/shard_map/all_gather | solution.py:52
  43.1 0.1 pad_maximum_fusion
  43.2 1.4 %multiply_subtract_fusion = (f32[8,16384]{1,0:T(8,128)}, f32[8,16384]{1,0:T(8,128)}, f32[8,16384]{1,0:T(8,128)}) fusion(f32[8,16384]{1,0:T(8,128)S(1)} %copy-done, f32[8,16384]{1,0:T(8,128)S(1)} %bitcast.35, f32[8,16384]{1,0:T(8,128)S(1)} %copy-done.1, f32[8,16384]{1,0:T(8,128)S(1)} %copy-done.2), kind=kLoop, calls=%fused_computation.4 | loop fusion | flops 1966080 | bytes 3670016 | tf_op jit(solution)/shard_map/sub | solution.py:22
  44.6 5.8 %all-to-all-done = bf16[32,8,256]{2,1,0:T(8,128)(2,1)S(1)} async-done(((bf16[32,8,256]{2,1,0:T(8,128)(2,1)}), bf16[32,8,256]{2,1,0:T(8,128)(2,1)S(1)}, u32[]{:S(2)}, u32[]{:S(2)}) %all-to-all-start) | async-done | bytes 131104 | tf_op jit(solution)/shard_map/all_to_all | solution.py:50
  50.5 3.4 %all_gather.37 = bf16[256,512]{1,0:T(8,128)(2,1)S(1)} all-gather(bf16[256,256]{1,0:T(8,128)(2,1)S(1)} %bitcast.41), channel_id=1, replica_groups={{0,32},{96,64},{128,160},{224,192},{288,256},{320,352},{416,384},{448,4..., dimensions={1}, use_global_device_ids=true | all-gather | bytes 393216 | tf_op jit(solution)/shard_map/all_gather | solution.py:57
  53.8 0.7 %copy.9 = bf16[256,512]{1,0:T(8,128)(2,1)} copy(bf16[256,512]{1,0:T(8,128)(2,1)S(1)} %all_gather.37) | data formatting | bytes 524288
  (5 shorter events, 0.2 us)
Async XLA Ops:
  19.5 11.7 %copy-start.2 = (f32[8,16384]{1,0:T(8,128)S(1)}, f32[8,16384]{1,0:T(8,128)}, u32[]{:S(2)}) copy-start(f32[8,16384]{1,0:T(8,128)} %param.7) | copy-start | bytes 1572868
  24.8 6.5 %copy-start.1 = (f32[8,16384]{1,0:T(8,128)S(1)}, f32[8,16384]{1,0:T(8,128)}, u32[]{:S(2)}) copy-start(f32[8,16384]{1,0:T(8,128)} %param.6) | copy-start | bytes 1572868
  24.8 6.5 %copy-start = (f32[8,16384]{1,0:T(8,128)S(1)}, f32[8,16384]{1,0:T(8,128)}, u32[]{:S(2)}) copy-start(f32[8,16384]{1,0:T(8,128)} %param.5) | copy-start | bytes 1572868
  32.2 18.2 %all-to-all-start = ((bf16[32,8,256]{2,1,0:T(8,128)(2,1)}), bf16[32,8,256]{2,1,0:T(8,128)(2,1)S(1)}, u32[]{:S(2)}, u32[]{:S(2)}) async-start(bf16[32,8,256]{2,1,0:T(8,128)(2,1)} %fusion.12), calls=%async_computation | async-start | bytes 262144 | tf_op jit(solution)/shard_map/all_to_all | solution.py:50

commit v7 on v5

--- a/solution.py
+++ b/solution.py
@@ -154,7 +154,8 @@
     mean_grad = lax.all_gather(mean_half, REP, axis_index_groups=chips)
     new_master, new_one, new_two = finish(mean_grad, master, moment_one, moment_two)
     moved, new_master, new_one, new_two = lax.optimization_barrier((moved, new_master, new_one, new_two))
-    rollout = lax.all_gather(moved.reshape(fresh.shape), REP, axis=1, tiled=True, axis_index_groups=chips)
+    sides = lax.all_gather(moved.reshape(fresh.shape), REP, axis_index_groups=chips)
+    rollout = jnp.concatenate([sides[0], sides[1]], 1)
     return (new_master, new_one, new_two, rollout)
 
 

time: 54.5 us -> 54.6 us (level)
  other arithmetic: 1.16 us -> 1.88 us
  local copies, waits for them, and re-layouts: 0.72 us -> 0.03 us
    concatenate x0 -> x1, other arithmetic: none -> 0.72 us  [local(): rollout = jnp.concatenate([sides[0], sides[1]], 1)]
    unnamed x7 -> x6, local copies, waits for them, and re-layouts: 0.72 us -> 0.02 us
where the time goes in v7:
time: 54.6 us; the launch traced here: 54.3 us
  blocking collectives  35 us (64%)
  starting transfers between devices  8.37 us (15%)
  waiting for transfers between devices  6.07 us (11%)
  Pallas kernels  2.3 us (4%)
  other arithmetic  1.88 us (3%)
  between operations  0.68 us (1%)
    all_gather x3, blocking collectives, local(): lines = lax.all_gather(total, REP, axis_index_groups=pairs)  20.5 us
    all_gather x1, blocking collectives, local(): total = combine(lax.all_gather(grads[0].astype(BF16), 'core'), owners)  8.69 us
    all_to_all x1, starting transfers between devices, local(): lax.all_to_all(fresh.reshape(owners, rows, -1), FSDP, split_axis=0, conca...  8.37 us
    all_to_all x1, waiting for transfers between devices, local(): lax.all_to_all(fresh.reshape(owners, rows, -1), FSDP, split_axis=0, conca...  6.07 us
    all_gather x1, blocking collectives, local(): lax.all_gather(moved.reshape(fresh.shape), REP, axis_index_groups=chips)  3.38 us
    all_gather x1, blocking collectives, local(): mean_grad = lax.all_gather(mean_half, REP, axis_index_groups=chips)  2.42 us
    pallas_call x1, Pallas kernels, finish(): pl.pallas_call(kernel, in_specs=[VMEM] * 4, out_specs=[pl.BlockSpec(memor...  1.34 us
  transfers between devices with their start and end apart: 1, of which 1 were waited for; matrix products, arithmetic and copies ran while one was open for 0% of the time, Pallas kernels for 2%

profile of v7, /device:TPU:1, one launch (start us, length us, event | category | flops | bytes accessed | tf_op | source)
XLA Modules:
  0.0 54.3 jit_solution(4914028820232097303)
XLA Ops:
  0.6 1.1 %convert_element_type.3 = bf16[1,8,16384]{2,1,0:T(8,128)(2,1)S(1)} convert(f32[1,8,16384]{2,1,0:T(8,128)} %param.4) | non-fusion elementwise | flops 131072 | bytes 786432 | tf_op jit(solution)/shard_map/convert_element_type | solution.py:145
  1.7 8.7 %all_gather.31.chips_ref = bf16[2,8,16384]{2,1,0:T(8,128)(2,1)S(1)} all-gather(bf16[1,8,16384]{2,1,0:T(8,128)(2,1)S(1)} %convert_element_type.3), channel_id=1, replica_groups=mesh['y_hi'=2,'x'=4,'core'=2,'z'=8,'y_lo'=4] {'core'}, dimensions={0}, use_global_device_ids=true | all-gather | bytes 786432 | tf_op jit(solution)/shard_map/all_gather | solution.py:145
  10.4 9.0 %all-gather = bf16[512,256]{1,0:T(8,128)(2,1)S(1)} all-gather(bf16[256,256]{1,0:T(8,128)(2,1)S(1)} %combine.1), channel_id=2, replica_groups={{0,96},{32,256},{64,352},{128,224},{160,384},{192,480},{288,320},{416,4..., dimensions={0}, use_global_device_ids=true | all-gather | bytes 393216 | tf_op jit(solution)/shard_map/all_gather | solution.py:148
  19.4 0.0 copy-start.2
  19.5 0.0 copy-start
  19.5 0.0 copy-start.1
  19.5 5.2 %all-gather.1 = bf16[512,256]{1,0:T(8,128)(2,1)S(1)} all-gather(bf16[256,256]{1,0:T(8,128)(2,1)S(1)} %reduce_sum.24), channel_id=3, replica_groups={{0,224},{32,64},{96,128},{160,192},{256,352},{288,448},{320,416},{384,4..., dimensions={0}, use_global_device_ids=true | all-gather | bytes 393216 | tf_op jit(solution)/shard_map/all_gather | solution.py:148
  24.7 6.3 %all-gather.2 = bf16[512,256]{1,0:T(8,128)(2,1)S(1)} all-gather(bf16[256,256]{1,0:T(8,128)(2,1)S(1)} %reduce_sum.25), channel_id=4, replica_groups={{0,288},{32,192},{64,160},{96,320},{128,416},{224,448},{256,480},{352,3..., dimensions={0}, use_global_device_ids=true | all-gather | bytes 393216 | tf_op jit(solution)/shard_map/all_gather | solution.py:148
  31.0 0.0 copy-done.2
  31.0 0.0 copy-done
  31.0 0.0 copy-done.1
  31.0 0.9 %begin.1 = (bf16[256,256]{1,0:T(8,128)(2,1)}, f32[256,256]{1,0:T(8,128)S(1)}) custom-call(bf16[2,256,256]{2,1,0:T(8,128)(2,1)S(1)} %bitcast.11, f32[8,16384]{1,0:T(8,128)S(1)} %copy-done, f32[8,16384]{1,0:T(8,128)S(1)} %copy-done.1, f32[8,16384]{1,0:T(8,128)S(1)} %copy-done.2), custom_call_target="tpu_custom_call" | custom-call | flops 1310720 | bytes 1310720 | tf_op jit(solution)/shard_map/begin/pallas_call | solution.py:83
  32.0 8.4 %all-to-all-start = ((bf16[32,8,256]{2,1,0:T(8,128)(2,1)}), bf16[32,8,256]{2,1,0:T(8,128)(2,1)S(1)}, u32[]{:S(2)}, u32[]{:S(2)}) async-start(bf16[32,8,256]{2,1,0:T(8,128)(2,1)} %bitcast.3), calls=%async_computation | async-start | bytes 262144 | tf_op jit(solution)/shard_map/all_to_all | solution.py:152
  40.3 2.4 %all-gather.3 = f32[512,256]{1,0:T(8,128)S(1)} all-gather(f32[256,256]{1,0:T(8,128)S(1)} %get-tuple-element.14), channel_id=5, replica_groups={{0,32},{96,64},{128,160},{224,192},{288,256},{320,352},{416,384},{448,4..., dimensions={0}, use_global_device_ids=true | all-gather | bytes 786432 | tf_op jit(solution)/shard_map/all_gather | solution.py:154
  42.8 1.3 %finish.1 = (f32[8,16384]{1,0:T(8,128)}, f32[8,16384]{1,0:T(8,128)}, f32[8,16384]{1,0:T(8,128)}) custom-call(f32[2,256,256]{2,1,0:T(8,128)S(1)} %bitcast.10, f32[8,16384]{1,0:T(8,128)S(1)} %copy-done, f32[8,16384]{1,0:T(8,128)S(1)} %copy-done.1, f32[8,16384]{1,0:T(8,128)S(1)} %copy-done.2), custom_call_target="tpu_custom_call" | custom-call | flops 2621440 | bytes 3670016 | tf_op jit(solution)/shard_map/finish/pallas_call | solution.py:126
  44.1 6.1 %all-to-all-done = bf16[32,8,256]{2,1,0:T(8,128)(2,1)S(1)} async-done(((bf16[32,8,256]{2,1,0:T(8,128)(2,1)}), bf16[32,8,256]{2,1,0:T(8,128)(2,1)S(1)}, u32[]{:S(2)}, u32[]{:S(2)}) %all-to-all-start) | async-done | bytes 131104 | tf_op jit(solution)/shard_map/all_to_all | solution.py:152
  50.2 3.4 %all_gather.40 = bf16[2,256,256]{2,1,0:T(8,128)(2,1)S(1)} all-gather(bf16[1,256,256]{2,1,0:T(8,128)(2,1)S(1)} %bitcast.14), channel_id=1, replica_groups={{0,32},{96,64},{128,160},{224,192},{288,256},{320,352},{416,384},{448,4..., dimensions={0}, use_global_device_ids=true | all-gather | bytes 393216 | tf_op jit(solution)/shard_map/all_gather | solution.py:157
  53.6 0.7 %pad_maximum_fusion = bf16[256,512]{1,0:T(8,128)(2,1)} fusion(bf16[256,256]{1,0:T(8,128)(2,1)S(1)} %get-tuple-element.23, bf16[256,256]{1,0:T(8,128)(2,1)S(1)} %get-tuple-element.22), kind=kLoop, calls=%fused_computation | loop fusion | flops 524288 | bytes 524288 | tf_op jit(solution)/shard_map/concatenate | solution.py:158
  (4 shorter events, 0.1 us)
Async XLA Ops:
  19.4 11.6 %copy-start.2 = (f32[8,16384]{1,0:T(8,128)S(1)}, f32[8,16384]{1,0:T(8,128)}, u32[]{:S(2)}) copy-start(f32[8,16384]{1,0:T(8,128)} %two_ref.3) | copy-start | bytes 1572868
  19.5 11.6 %copy-start = (f32[8,16384]{1,0:T(8,128)S(1)}, f32[8,16384]{1,0:T(8,128)}, u32[]{:S(2)}) copy-start(f32[8,16384]{1,0:T(8,128)} %master_ref.3) | copy-start | bytes 1572868
  19.5 11.6 %copy-start.1 = (f32[8,16384]{1,0:T(8,128)S(1)}, f32[8,16384]{1,0:T(8,128)}, u32[]{:S(2)}) copy-start(f32[8,16384]{1,0:T(8,128)} %one_ref.3) | copy-start | bytes 1572868
  32.0 18.2 %all-to-all-start = ((bf16[32,8,256]{2,1,0:T(8,128)(2,1)}), bf16[32,8,256]{2,1,0:T(8,128)(2,1)S(1)}, u32[]{:S(2)}, u32[]{:S(2)}) async-start(bf16[32,8,256]{2,1,0:T(8,128)(2,1)} %bitcast.3), calls=%async_computation | async-start | bytes 262144 | tf_op jit(solution)/shard_map/all_to_all | solution.py:152
